TPU v7x, 512 devices: a whole 4x4x16 slice. The times are simulated.
512 devices in a mesh: dp: 16 (over z_lo, x), expert: 32 (over y, z_hi, core).
Axes of the slice: x: 4, y: 4, z: 16 (z_hi: 4, z_lo: 4; z = z_hi * 4 + z_lo), core: 2. Of those that a mesh axis runs over, the one named last changes fastest.
Arguments:
- tokens: bfloat16 [65536, 2560], P(('dp', 'expert')), may hold values from -6 to 6
- cotangent: bfloat16 [65536, 2560], P(('dp', 'expert')), may hold values from -6 to 6
- expert_ids: int32 [65536, 2], P(('dp', 'expert')), may hold values from 0 to 31, all different within a row; in each aligned block of 128 rows (0 to 127, 128 to 255, ...) at most 9 rows name the same one
- gate_values: float32 [65536, 2], P(('dp', 'expert')), may hold values from 0.05 to 1
- w_gate: bfloat16 [32, 768, 2560], P('expert', 'dp'), may hold values from -0.125 to 0.125
- w_up: bfloat16 [32, 768, 2560], P('expert', 'dp'), may hold values from -0.125 to 0.125
- w_down: bfloat16 [32, 768, 2560], P('expert', 'dp'), may hold values from -0.21875 to 0.21875
Outputs:
- token_grad: bfloat16 [65536, 2560], P(('dp', 'expert'))
- gate_grad: float32 [65536, 2], P(('dp', 'expert'))
Inputs may be any that keep to these rules, and one draw needn't show every extreme that they name: `expert_ids`: each row names 2 different experts. Among the rows of one device (128 aligned rows), no expert is named by more than 9 rows, and in some blocks one expert is named by exactly 9.
All inputs are finite; a program needn't handle non-finite values.
Results may differ from a plain program's by a relative error of at most 0.02.
Values may be sent and summed in bfloat16 or wider, within the bound.
No kernel may reach another device: no remote copies, remote signals or barrier semaphores. Data moves between devices by JAX's collectives and lax.ppermute only.
A program may use at most 128 MiB of HBM per device.

v0:
```python
import jax
import jax.numpy as jnp
from jax import lax
from jax.sharding import PartitionSpec as P


def front_half(rows_x, wg, wu):
    pre_gate = jnp.einsum("erd,efd->erf", rows_x, wg, preferred_element_type=jnp.float32)
    pre_up = jnp.einsum("erd,efd->erf", rows_x, wu, preferred_element_type=jnp.float32)
    sigma = jax.nn.sigmoid(pre_gate)
    hidden = (pre_gate * sigma * pre_up).astype(jnp.bfloat16)
    return (pre_gate, pre_up, sigma, hidden)


def back_half(scaled, pre_gate, pre_up, sigma, hidden, wg, wu, wd):
    expert_out = jnp.einsum("erf,efd->erd", hidden, wd, preferred_element_type=jnp.float32)
    grad_hidden = jnp.einsum("erd,efd->erf", scaled, wd, preferred_element_type=jnp.float32)
    grad_gate_pre = (grad_hidden * pre_up * sigma * (1.0 + pre_gate * (1.0 - sigma))).astype(
        jnp.bfloat16
    )
    grad_up_pre = (grad_hidden * pre_gate * sigma).astype(jnp.bfloat16)
    back = jnp.einsum("erf,efd->erd", grad_gate_pre, wg, preferred_element_type=jnp.float32)
    back = back + jnp.einsum("erf,efd->erd", grad_up_pre, wu, preferred_element_type=jnp.float32)
    return (expert_out, back)


def local(tokens, cotangent, expert_ids, gate_values, w_gate, w_up, w_down):
    tok_rows = tokens.shape[0]
    top = expert_ids.shape[1]
    local_experts = w_gate.shape[0]
    experts = local_experts * lax.axis_size("expert")
    slots = min(tok_rows, max(2, 9 * tok_rows * top // (8 * experts)))
    width_k = tok_rows * top
    flat = expert_ids.reshape(width_k)
    onehot = (flat[:, None] == jnp.arange(experts, dtype=jnp.int32)[None, :]).astype(jnp.int32)
    before = jnp.cumsum(onehot, axis=0) - onehot
    slot = jnp.sum(before * onehot, axis=1)
    place = flat * slots + slot
    chosen = place[None, :] == jnp.arange(experts * slots, dtype=jnp.int32)[:, None]
    source = jnp.sum(jnp.where(chosen, jnp.arange(width_k, dtype=jnp.int32)[None, :], 0), axis=1)
    valid = jnp.any(chosen, axis=1)
    owner = source // top
    send_x = jnp.where(valid[:, None], tokens[owner], jnp.zeros((), jnp.bfloat16)).reshape(
        experts, slots, -1
    )
    send_dy = jnp.where(valid[:, None], cotangent[owner], jnp.zeros((), jnp.bfloat16)).reshape(
        experts, slots, -1
    )
    send_g = jnp.where(valid, gate_values.reshape(width_k)[source], jnp.float32(0.0)).reshape(
        experts, slots
    )
    rows_x, rows_dy, rows_g = (
        lax.all_to_all(send_x, "expert", split_axis=0, concat_axis=1, tiled=True),
        lax.all_to_all(send_dy, "expert", split_axis=0, concat_axis=1, tiled=True),
        lax.all_to_all(
            send_g.astype(jnp.bfloat16), "expert", split_axis=0, concat_axis=1, tiled=True
        ).astype(send_g.dtype),
    )
    scaled = (rows_g[..., None] * rows_dy.astype(jnp.float32)).astype(jnp.bfloat16)
    wg, wu, wd = (
        lax.all_gather(w_gate, "dp", axis=1, tiled=True),
        lax.all_gather(w_up, "dp", axis=1, tiled=True),
        lax.all_gather(w_down, "dp", axis=1, tiled=True),
    )
    pre_gate, pre_up, sigma, hidden = front_half(rows_x, wg, wu)
    expert_out, back = back_half(scaled, pre_gate, pre_up, sigma, hidden, wg, wu, wd)
    gate_term = jnp.sum(expert_out * rows_dy.astype(jnp.float32), axis=-1)
    row_grad = back.astype(jnp.bfloat16)
    home_grad, home_gate = (
        lax.all_to_all(row_grad, "expert", split_axis=1, concat_axis=0, tiled=True),
        lax.all_to_all(
            gate_term.astype(jnp.bfloat16), "expert", split_axis=1, concat_axis=0, tiled=True
        ).astype(gate_term.dtype),
    )
    picked = home_grad.reshape(experts * slots, -1)[place].astype(jnp.float32)
    token_grad = jnp.sum(picked.reshape(tok_rows, top, -1), axis=1).astype(jnp.bfloat16)
    gate_grad = home_gate.reshape(experts * slots)[place].reshape(tok_rows, top)
    return (token_grad, gate_grad)


def solution(mesh):
    return jax.shard_map(
        local,
        mesh=mesh,
        in_specs=(
            P(("dp", "expert"), None),
            P(("dp", "expert"), None),
            P(("dp", "expert"), None),
            P(("dp", "expert"), None),
            P("expert", "dp", None),
            P("expert", "dp", None),
            P("expert", "dp", None),
        ),
        out_specs=(P(("dp", "expert"), None), P(("dp", "expert"), None)),
        check_vma=False,
    )
```

profile of v0, /device:TPU:1, one launch (start us, length us, event | category | flops | bytes accessed | tf_op | source)
XLA Modules:
  0.0 598.2 jit_solution(11852661637790657408)
XLA Ops:
  11.8 2.4 gather_fusion
  15.1 19.4 %all-to-all-start = ((bf16[32,1,9]{2,1,0:T(2,128)(2,1)}), bf16[32,1,9]{2,1,0:T(2,128)(2,1)S(1)}, u32[]{:S(2)}, u32[]{:S(2)}) async-start(bf16[32,1,9]{2,1,0:T(2,128)(2,1)} %convert_element_type.149), calls=%async_computation | async-start | bytes 32768 | tf_op jit(solution)/shard_map/all_to_all | solution.py:55
  34.6 2.6 gather_fusion.1
  37.2 1.9 gather.23
  39.1 3.1 gather_fusion.2
  42.2 3.2 gather.25
  45.4 4.5 broadcast_select_fusion.1
  49.9 14.6 %all-to-all-start.1 = ((bf16[32,9,2560]{2,1,0:T(8,128)(2,1)}), bf16[32,9,2560]{2,1,0:T(8,128)(2,1)S(1)}, u32[]{:S(2)}, u32[]{:S(2)}) async-start(bf16[32,9,2560]{2,1,0:T(8,128)(2,1)} %get-tuple-element.12), calls=%async_computation.1 | async-start | bytes 5242880 | tf_op jit(solution)/shard_map/all_to_all | solution.py:54
  65.2 90.7 %all-to-all-done.1 = bf16[32,9,2560]{2,1,0:T(8,128)(2,1)S(1)} async-done(((bf16[32,9,2560]{2,1,0:T(8,128)(2,1)}), bf16[32,9,2560]{2,1,0:T(8,128)(2,1)S(1)}, u32[]{:S(2)}, u32[]{:S(2)}) %all-to-all-start.1) | async-done | bytes 1474592 | tf_op jit(solution)/shard_map/all_to_all | solution.py:54
  155.9 56.4 %all-to-all-start.2 = ((bf16[32,9,2560]{2,1,0:T(8,128)(2,1)}), bf16[32,9,2560]{2,1,0:T(8,128)(2,1)}, u32[]{:S(2)}, u32[]{:S(2)}) async-start(bf16[32,9,2560]{2,1,0:T(8,128)(2,1)} %get-tuple-element.13), calls=%async_computation.2 | async-start | bytes 5242880 | tf_op jit(solution)/shard_map/all_to_all | solution.py:53
  212.5 1.9 reshape.349
  214.4 2.0 reshape.348
  216.3 81.2 %all-to-all-done.2 = bf16[32,9,2560]{2,1,0:T(8,128)(2,1)} async-done(((bf16[32,9,2560]{2,1,0:T(8,128)(2,1)}), bf16[32,9,2560]{2,1,0:T(8,128)(2,1)}, u32[]{:S(2)}, u32[]{:S(2)}) %all-to-all-start.2) | async-done | bytes 1474592 | tf_op jit(solution)/shard_map/all_to_all | solution.py:53
  297.5 2.0 reshape.342
  299.6 3.5 fusion.3
  303.1 51.0 %all-gather.6.cloned.1.call-done = bf16[1,768,2560]{2,1,0:T(8,128)(2,1)} async-done(((bf16[1,48,2560]{2,1,0:T(8,128)(2,1)}), bf16[1,768,2560]{2,1,0:T(8,128)(2,1)}) %all-gather.6.cloned.1.call-update) | async-done | bytes 3932176 | tf_op jit(solution)/shard_map/all_gather | solution.py:62
  354.1 4.4 fusion.6
  358.5 84.1 %all-gather.4.cloned.1.call-done = bf16[1,768,2560]{2,1,0:T(8,128)(2,1)} async-done(((bf16[1,48,2560]{2,1,0:T(8,128)(2,1)}), bf16[1,768,2560]{2,1,0:T(8,128)(2,1)}) %all-gather.4.cloned.1.call-update) | async-done | bytes 3932176 | tf_op jit(solution)/shard_map/all_gather | solution.py:63
  442.6 4.8 fusion.14
  448.1 23.5 %all-to-all-start.4 = ((bf16[1,32,9]{2,0,1:T(2,128)(2,1)}), bf16[1,32,9]{2,0,1:T(2,128)(2,1)S(1)}, u32[]{:S(2)}, u32[]{:S(2)}) async-start(bf16[1,32,9]{2,0,1:T(2,128)(2,1)} %convert_element_type.150), calls=%async_computation.4 | async-start | bytes 32768 | tf_op jit(solution)/shard_map/all_to_all | solution.py:71
  471.6 4.5 fusion.9
  476.2 1.5 fusion.1
  479.7 3.9 copy.48
  484.0 10.9 %reduce.17 = bf16[288,2560]{1,0:T(8,128)(2,1)S(1)} reduce(bf16[288,1,2560]{2,1,0:T(2,128)(2,1)} %bitcast.55, bf16[]{:T(256)} %broadcast.219), dimensions={1}, to_apply=%bitcast.53.reduce_sub_computation | reduce | bytes 2949122
  494.9 1.6 reshape.406
  496.5 14.6 %all-to-all-start.3 = ((bf16[32,2,11520]{2,1,0:T(2,128)(2,1)}), bf16[32,2,11520]{2,1,0:T(2,128)(2,1)S(1)}, u32[]{:S(2)}, u32[]{:S(2)}) async-start(bf16[32,2,11520]{2,1,0:T(2,128)(2,1)} %reshape.406), calls=%async_computation.3 | async-start | bytes 2949120 | tf_op jit(solution)/shard_map/all_to_all | solution.py:70
  511.6 1.9 gather_fusion.4
  514.3 65.3 %all-to-all-done.3 = bf16[32,2,11520]{2,1,0:T(2,128)(2,1)S(1)} async-done(((bf16[32,2,11520]{2,1,0:T(2,128)(2,1)}), bf16[32,2,11520]{2,1,0:T(2,128)(2,1)S(1)}, u32[]{:S(2)}, u32[]{:S(2)}) %all-to-all-start.3) | async-done | bytes 1474592 | tf_op jit(solution)/shard_map/all_to_all | solution.py:70
  579.6 3.7 reshape.407
  583.2 2.0 copy.47
  585.3 1.4 gather_fusion.3
  587.3 4.4 reduce_sum.47
  (57 shorter events, 11.5 us)
Async XLA Ops:
  7.2 27.4 %copy-start = (bf16[128,2560]{1,0:T(8,128)(2,1)S(1)}, bf16[128,2560]{1,0:T(8,128)(2,1)}, u32[]{:S(2)}) copy-start(bf16[128,2560]{1,0:T(8,128)(2,1)} %param.8) | copy-start | bytes 1966084
  7.2 292.4 %all-gather.8.cloned.1.call-start = ((), (), s32[]{:S(2)}) async-start(), calls=%async_computation.7 | async-start | bytes 4177920 | tf_op jit(solution)/shard_map/all_gather | solution.py:61
  7.9 346.2 %all-gather.6.cloned.1.call-start = ((), (), s32[]{:S(2)}) async-start(), calls=%async_computation.6 | async-start | bytes 4177920 | tf_op jit(solution)/shard_map/all_gather | solution.py:62
  15.1 34.8 %all-to-all-start = ((bf16[32,1,9]{2,1,0:T(2,128)(2,1)}), bf16[32,1,9]{2,1,0:T(2,128)(2,1)S(1)}, u32[]{:S(2)}, u32[]{:S(2)}) async-start(bf16[32,1,9]{2,1,0:T(2,128)(2,1)} %convert_element_type.149), calls=%async_computation | async-start | bytes 32768 | tf_op jit(solution)/shard_map/all_to_all | solution.py:55
  37.2 1.9 copy-start.1
  42.2 3.2 copy-start.2
  49.9 106.0 %all-to-all-start.1 = ((bf16[32,9,2560]{2,1,0:T(8,128)(2,1)}), bf16[32,9,2560]{2,1,0:T(8,128)(2,1)S(1)}, u32[]{:S(2)}, u32[]{:S(2)}) async-start(bf16[32,9,2560]{2,1,0:T(8,128)(2,1)} %get-tuple-element.12), calls=%async_computation.1 | async-start | bytes 5242880 | tf_op jit(solution)/shard_map/all_to_all | solution.py:54
  64.5 378.1 %all-gather.4.cloned.1.call-start = ((), (), s32[]{:S(2)}) async-start(), calls=%async_computation.5 | async-start | bytes 4177920 | tf_op jit(solution)/shard_map/all_gather | solution.py:63
  155.9 141.6 %all-to-all-start.2 = ((bf16[32,9,2560]{2,1,0:T(8,128)(2,1)}), bf16[32,9,2560]{2,1,0:T(8,128)(2,1)}, u32[]{:S(2)}, u32[]{:S(2)}) async-start(bf16[32,9,2560]{2,1,0:T(8,128)(2,1)} %get-tuple-element.13), calls=%async_computation.2 | async-start | bytes 5242880 | tf_op jit(solution)/shard_map/all_to_all | solution.py:53
  448.1 48.4 %all-to-all-start.4 = ((bf16[1,32,9]{2,0,1:T(2,128)(2,1)}), bf16[1,32,9]{2,0,1:T(2,128)(2,1)S(1)}, u32[]{:S(2)}, u32[]{:S(2)}) async-start(bf16[1,32,9]{2,0,1:T(2,128)(2,1)} %convert_element_type.150), calls=%async_computation.4 | async-start | bytes 32768 | tf_op jit(solution)/shard_map/all_to_all | solution.py:71
  471.6 4.5 copy-start.4
  471.6 4.5 copy-start.6
  476.1 2.1 copy-start.5
  494.9 16.2 %copy-start.3 = (s32[128,2]{0,1:T(2,128)S(1)}, s32[128,2]{0,1:T(2,128)}, u32[]{:S(2)}) copy-start(s32[128,2]{0,1:T(2,128)} %param.9) | copy-start | bytes 3076
  496.5 83.1 %all-to-all-start.3 = ((bf16[32,2,11520]{2,1,0:T(2,128)(2,1)}), bf16[32,2,11520]{2,1,0:T(2,128)(2,1)S(1)}, u32[]{:S(2)}, u32[]{:S(2)}) async-start(bf16[32,2,11520]{2,1,0:T(2,128)(2,1)} %reshape.406), calls=%async_computation.3 | async-start | bytes 2949120 | tf_op jit(solution)/shard_map/all_to_all | solution.py:70
Sparse Core Ops, SparseCore 0:
  10.1 130.7 all-gather.7
  142.9 211.1 all-gather.5
  356.2 86.3 all-gather.3
where the time goes:
time: 599 us; the launch traced here: 598 us
  waiting for transfers between devices  374 us (62%)
  starting transfers between devices  129 us (22%)
  local copies, waits for them, and re-layouts  40.2 us (7%)
  other arithmetic  21 us (4%)
  matrix products  20 us (3%)
  between operations  14.1 us (2%)
    all_to_all x1, waiting for transfers between devices, local(): lax.all_to_all(send_dy, 'expert', split_axis=0, concat_axis=1, tiled=True)  90.7 us
    all_gather x1, waiting for transfers between devices, local(): lax.all_gather(w_down, 'dp', axis=1, tiled=True)  84.1 us
    all_to_all x1, waiting for transfers between devices, local(): lax.all_to_all(send_x, 'expert', split_axis=0, concat_axis=1, tiled=True)  81.2 us
    all_to_all x1, waiting for transfers between devices, local(): lax.all_to_all(row_grad, 'expert', split_axis=1, concat_axis=0, tiled=True)  65.3 us
    all_to_all x1, starting transfers between devices, local(): lax.all_to_all(send_x, 'expert', split_axis=0, concat_axis=1, tiled=True)  56.4 us
    all_gather x1, waiting for transfers between devices, local(): lax.all_gather(w_up, 'dp', axis=1, tiled=True)  51 us
    all_to_all x1, starting transfers between devices, local(): lax.all_to_all(gate_term.astype(jnp.bfloat16), 'expert', split_axis=1, co...  23.5 us
    all_to_all x1, starting transfers between devices, local(): lax.all_to_all(send_g.astype(jnp.bfloat16), 'expert', split_axis=0, conca...  19.4 us
  transfers between devices with their start and end apart: 8, of which 5 were waited for; matrix products, arithmetic and copies ran while one was open for 11% of the time, Pallas kernels for 0%

commit v1 on v0

v1 whole, which is shorter than its diff:
```python
import functools

import jax
import jax.numpy as jnp
from jax import lax
from jax.experimental import pallas as pl
from jax.experimental.pallas import tpu as pltpu
from jax.sharding import Mesh, PartitionSpec as P

AXES = ("zl", "x", "y", "zh", "c")
PLANE = ("y", "x", "c")
RING = ("zh", "zl")
SIZES = (4, 4, 4, 4, 2)
F32 = jnp.float32
BF16 = jnp.bfloat16

SHIFT = ((-6, 0, 0, 6), (-4, -2, 2, 4), (-2, -4, 4, 2), (0, -6, 6, 0))


def flat_index(zl, x, y, zh, c):
    return (((zl * 4 + x) * 4 + y) * 4 + zh) * 2 + c


def spread_pairs():
    pairs = []
    for zl in range(4):
        for x in range(4):
            for y in range(4):
                for zh in range(4):
                    for c in range(2):
                        z = (zh * 4 + zl + SHIFT[x][zl]) % 16
                        pairs.append(
                            (flat_index(zl, x, y, zh, c), flat_index(z % 4, zh, y, z // 4, c))
                        )
    return pairs


def dot_t(a, b):
    return lax.dot_general(a, b, (((1,), (1,)), ((), ())), preferred_element_type=F32)


def expert_kernel(steps, width, rows_ref, w_ref, out_ref, acc, gate):
    step = pl.program_id(0)
    slabs, height, _ = w_ref.shape
    third = height // 3
    hid = slabs * third
    x = rows_ref[:, :width]
    dy = rows_ref[:, width:]
    wg = w_ref[:, 0:third, :].reshape(hid, width)
    wu = w_ref[:, third : 2 * third, :].reshape(hid, width)
    wd = w_ref[:, 2 * third : 3 * third, :].reshape(hid, width)
    pre_gate = dot_t(x, wg)
    pre_up = dot_t(x, wu)
    q = dot_t(dy, wd)
    sigma = jax.nn.sigmoid(pre_gate)
    act = pre_gate * sigma
    hidden = (act * pre_up).astype(BF16).astype(F32)
    grad_gate = (q * pre_up * sigma * (1.0 + pre_gate * (1.0 - sigma))).astype(BF16)
    grad_up = (q * act).astype(BF16)
    back = jnp.dot(grad_gate, wg, preferred_element_type=F32)
    back = back + jnp.dot(grad_up, wu, preferred_element_type=F32)
    term = jnp.sum(hidden * q, axis=1, keepdims=True)

    @pl.when(step == 0)
    def _():
        acc[...] = back
        gate[...] = term

    @pl.when(step > 0)
    def _():
        acc[...] += back
        gate[...] += term

    @pl.when(step == steps - 1)
    def _():
        out_ref[:, :width] = acc[...].astype(BF16)
        whole = gate[...]
        high = whole.astype(BF16).astype(F32)
        lane = lax.broadcasted_iota(jnp.int32, (whole.shape[0], 128), 1)
        tail = jnp.where(lane == 0, high, jnp.where(lane == 1, whole - high, 0.0))
        out_ref[:, width:] = tail.astype(BF16)


def expert_layer(rows, slabs):
    count, wide = rows.shape
    width = wide // 2
    planes, height, _ = slabs.shape
    steps = 4
    return pl.pallas_call(
        functools.partial(expert_kernel, steps, width),
        grid=(steps,),
        out_shape=jax.ShapeDtypeStruct((count, width + 128), BF16),
        in_specs=[
            pl.BlockSpec((count, wide), lambda i: (0, 0)),
            pl.BlockSpec((planes // steps, height, width), lambda i: (i, 0, 0)),
        ],
        out_specs=pl.BlockSpec((count, width + 128), lambda i: (0, 0)),
        scratch_shapes=[pltpu.VMEM((count, width), F32), pltpu.VMEM((count, 1), F32)],
        compiler_params=pltpu.CompilerParams(vmem_limit_bytes=48 * 1024 * 1024),
    )(rows, slabs)


def local(tokens, cotangent, expert_ids, gate_values, w_gate, w_up, w_down):
    tok_rows, width = tokens.shape
    experts, slots = 32, 9
    places = experts * slots

    slab = jnp.concatenate([w_gate[0], w_up[0], w_down[0]], axis=0)
    slab = lax.ppermute(slab, AXES, spread_pairs())
    slabs = lax.all_gather(slab, RING, axis=0, tiled=False)

    names = jnp.arange(experts, dtype=jnp.int32)
    pick = (expert_ids[:, :, None] == names[None, None, :]).astype(F32)
    member = jnp.sum(pick, axis=1)
    row = jnp.arange(tok_rows, dtype=jnp.int32)
    earlier = (row[None, :] < row[:, None]).astype(BF16)
    before = jnp.dot(earlier, member.astype(BF16), preferred_element_type=F32)
    slot = jnp.sum(before[:, None, :] * pick, axis=2).astype(jnp.int32)
    place = expert_ids * slots + slot
    spots = jnp.arange(places, dtype=jnp.int32)
    send_pick = (
        (place[:, 0][None, :] == spots[:, None]) | (place[:, 1][None, :] == spots[:, None])
    ).astype(BF16)
    both = jnp.concatenate([tokens, cotangent], axis=1)
    send = jnp.dot(send_pick, both, preferred_element_type=F32).astype(BF16)
    rows = lax.all_to_all(
        send.reshape(experts, slots, 2 * width), PLANE, split_axis=0, concat_axis=0, tiled=True
    )

    back = expert_layer(rows.reshape(places, 2 * width), slabs)
    home = lax.all_to_all(
        back.reshape(experts, slots, width + 128), PLANE, split_axis=0, concat_axis=0, tiled=True
    ).reshape(places, width + 128)

    first = (place[:, 0][:, None] == spots[None, :]).astype(F32)
    second = (place[:, 1][:, None] == spots[None, :]).astype(F32)
    weight = first * gate_values[:, 0:1] + second * gate_values[:, 1:2]
    high = weight.astype(BF16)
    low = (weight - high.astype(F32)).astype(BF16)
    grads = home[:, :width]
    token_grad = jnp.dot(high, grads, preferred_element_type=F32)
    token_grad = token_grad + jnp.dot(low, grads, preferred_element_type=F32)
    terms = home[:, width:]
    gates = [
        jnp.sum(jnp.dot(hot.astype(BF16), terms, preferred_element_type=F32), axis=1)
        for hot in (first, second)
    ]
    return token_grad.astype(BF16), jnp.stack(gates, axis=1)


def solution(mesh):
    fine = Mesh(mesh.devices.reshape(SIZES), AXES)
    rows = P(AXES, None)
    weights = P(("y", "zh", "c"), ("zl", "x"), None)
    return jax.shard_map(
        local,
        mesh=fine,
        in_specs=(rows, rows, rows, rows, weights, weights, weights),
        out_specs=(rows, rows),
        check_vma=False,
    )
```

time: 599 us -> 276 us (0.46)
  waiting for transfers between devices: 374 us -> 119 us
  starting transfers between devices: 129 us -> 23.1 us
  blocking collectives: 0 us -> 78.2 us
  local copies, waits for them, and re-layouts: 40.2 us -> 16.2 us
  other arithmetic: 21 us -> 1.85 us
  Pallas kernels: 0 us -> 17.8 us
  matrix products: 20 us -> 4.88 us
    all_to_all x5 -> x1, waiting for transfers between devices: 237 us -> 35 us  [local(): lax.all_to_all(back.reshape(experts, slots, width + 128), PLANE, split_ax...]
    all_to_all x5 -> x1, starting transfers between devices: 128 us -> 7.7 us  [local(): lax.all_to_all(back.reshape(experts, slots, width + 128), PLANE, split_ax...]
    all_to_all x0 -> x1, blocking collectives: none -> 78.2 us  [local(): lax.all_to_all(send.reshape(experts, slots, 2 * width), PLANE, split_axis...]
    all_gather x3 -> x1, waiting for transfers between devices: 135 us -> 63.3 us  [local(): slabs = lax.all_gather(slab, RING, axis=0, tiled=False)]
    ppermute x0 -> x1, waiting for transfers between devices: none -> 20.6 us  [local(): slab = lax.ppermute(slab, AXES, spread_pairs())]
    pallas_call x0 -> x1, Pallas kernels: none -> 17.8 us  [expert_layer(): pl.pallas_call(functools.partial(expert_kernel, steps, width), grid=(step...]
    gather x8 -> x0, local copies, waits for them, and re-layouts: 17 us -> none  [the longest x2 6.25 us: local(): tokens[owner]]
    ppermute x0 -> x1, starting transfers between devices: none -> 15.4 us  [local(): slab = lax.ppermute(slab, AXES, spread_pairs())]
  transfers between devices with their start and end apart: 8 -> 3, of which waited for: 5 -> 3; matrix products, arithmetic and copies ran while one was open for 11% -> 4% of each run, Pallas kernels for 0% -> 0%
where the time goes in v1:
time: 276 us; the launch traced here: 275 us
  waiting for transfers between devices  119 us (43%)
  blocking collectives  78.2 us (28%)
  starting transfers between devices  23.1 us (8%)
  Pallas kernels  17.8 us (6%)
  local copies, waits for them, and re-layouts  16.2 us (6%)
  between operations  14.2 us (5%)
  matrix products  4.88 us (2%)
    all_to_all x1, blocking collectives, local(): lax.all_to_all(send.reshape(experts, slots, 2 * width), PLANE, split_axis...  78.2 us
    all_gather x1, waiting for transfers between devices, local(): slabs = lax.all_gather(slab, RING, axis=0, tiled=False)  63.3 us
    all_to_all x1, waiting for transfers between devices, local(): lax.all_to_all(back.reshape(experts, slots, width + 128), PLANE, split_ax...  35 us
    ppermute x1, waiting for transfers between devices, local(): slab = lax.ppermute(slab, AXES, spread_pairs())  20.6 us
    pallas_call x1, Pallas kernels, expert_layer(): pl.pallas_call(functools.partial(expert_kernel, steps, width), grid=(step...  17.8 us
    ppermute x1, starting transfers between devices, local(): slab = lax.ppermute(slab, AXES, spread_pairs())  15.4 us
    all_to_all x1, starting transfers between devices, local(): lax.all_to_all(back.reshape(experts, slots, width + 128), PLANE, split_ax...  7.7 us
  transfers between devices with their start and end apart: 3, of which 3 were waited for; matrix products, arithmetic and copies ran while one was open for 4% of the time, Pallas kernels for 0%

profile of v1, /device:TPU:1, one launch (start us, length us, event | category | flops | bytes accessed | tf_op | source)
XLA Modules:
  0.0 275.1 jit_solution(3347437699846353139)
XLA Ops:
  7.2 0.0 copy-start.2
  7.2 0.0 all-gather.3.cloned.1.call-start
  7.2 1.2 pad_maximum_fusion
  8.5 15.4 %collective-permute-start = (bf16[144,2560]{1,0:T(8,128)(2,1)S(1)}, bf16[144,2560]{1,0:T(8,128)(2,1)S(1)}, u32[]{:S(2)}, u32[]{:S(2)}) collective-permute-start(bf16[144,2560]{1,0:T(8,128)(2,1)S(1)} %pad_maximum_fusion), channel_id=1, source_target_pairs={{0,260},{1,261},{2,294},{3,295},{4,320},{5,321},{6,354},{7,355},{8... | collective-permute-start | bytes 2211848 | tf_op jit(solution)/shard_map/ppermute | solution.py:109
  23.8 20.6 %collective-permute-done = bf16[144,2560]{1,0:T(8,128)(2,1)S(1)} collective-permute-done((bf16[144,2560]{1,0:T(8,128)(2,1)S(1)}, bf16[144,2560]{1,0:T(8,128)(2,1)S(1)}, u32[]{:S(2)}, u32[]{:S(2)}) %collective-permute-start) | collective-permute-done | bytes 737312 | tf_op jit(solution)/shard_map/ppermute | solution.py:109
  44.4 0.0 copy-start.1
  44.4 0.9 copy-done.1
  45.3 0.0 all-gather.3.cloned.1.call-update
  45.3 0.0 copy-done.2
  45.4 0.1 fusion.21
  45.6 2.2 convolution_convert_fusion
  47.8 3.4 %reshape.20 = bf16[32,9,5120]{2,1,0:T(8,128)(2,1)} reshape(bf16[288,5120]{1,0:T(8,128)(2,1)S(1)} %convolution_convert_fusion) | data formatting | bytes 5898240 | tf_op jit(solution)/shard_map/reshape | solution.py:127
  51.1 78.2 %all_to_all.10 = bf16[32,9,5120]{2,1,0:T(8,128)(2,1)} all-to-all(bf16[32,9,5120]{2,1,0:T(8,128)(2,1)} %reshape.20), channel_id=1, replica_groups=mesh['zl'=4,'x'=4,'y'=4,'zh'=4,'c'=2] {'y','x','c'}, dimensions={0} | all-to-all | bytes 5898240 | tf_op jit(solution)/shard_map/all_to_all | solution.py:126
  129.3 3.9 %reshape.21.rows_ref = bf16[288,5120]{1,0:T(8,128)(2,1)S(1)} reshape(bf16[32,9,5120]{2,1,0:T(8,128)(2,1)} %all_to_all.10) | data formatting | bytes 5898240 | tf_op jit(solution)/shard_map/reshape | solution.py:130
  133.2 63.3 %all-gather.3.cloned.1.call-done = bf16[2304,2560]{1,0:T(8,128)(2,1)} async-done(((bf16[144,2560]{1,0:T(8,128)(2,1)}), bf16[2304,2560]{1,0:T(8,128)(2,1)}) %all-gather.3.cloned.1.call-update) | async-done | bytes 11796496 | tf_op jit(solution)/shard_map/all_gather | solution.py:110
  196.6 17.8 %shard_map.86 = bf16[288,2688]{1,0:T(8,128)(2,1)S(1)} custom-call(bf16[288,5120]{1,0:T(8,128)(2,1)S(1)} %reshape.21.rows_ref, bf16[16,144,2560]{2,1,0:T(8,128)(2,1)} %bitcast.15), custom_call_target="tpu_custom_call" | custom-call | tf_op jit(solution)/shard_map/pallas_call | solution.py:89
  214.4 0.0 copy-start
  214.4 1.1 copy-done
  215.5 4.0 %reshape.22 = bf16[32,9,2688]{2,1,0:T(8,128)(2,1)} reshape(bf16[288,2688]{1,0:T(8,128)(2,1)} %copy-done) | data formatting | bytes 3096576 | tf_op jit(solution)/shard_map/reshape | solution.py:132
  219.6 0.0 copy-start.3
  219.6 7.7 %all-to-all-start.1 = ((bf16[32,9,2688]{2,1,0:T(8,128)(2,1)}), bf16[32,9,2688]{2,1,0:T(8,128)(2,1)}, u32[]{:S(2)}, u32[]{:S(2)}) async-start(bf16[32,9,2688]{2,1,0:T(8,128)(2,1)} %reshape.22), calls=%async_computation.1 | async-start | bytes 5505024 | tf_op jit(solution)/shard_map/all_to_all | solution.py:131
  227.3 0.0 copy-done.3
  227.3 35.0 %all-to-all-done.1 = bf16[32,9,2688]{2,1,0:T(8,128)(2,1)} async-done(((bf16[32,9,2688]{2,1,0:T(8,128)(2,1)}), bf16[32,9,2688]{2,1,0:T(8,128)(2,1)}, u32[]{:S(2)}, u32[]{:S(2)}) %all-to-all-start.1) | async-done | bytes 1548320 | tf_op jit(solution)/shard_map/all_to_all | solution.py:131
  262.3 2.8 %reshape.23 = bf16[288,2688]{1,0:T(8,128)(2,1)S(1)} reshape(bf16[32,9,2688]{2,1,0:T(8,128)(2,1)} %all-to-all-done.1) | data formatting | bytes 3096576 | tf_op jit(solution)/shard_map/reshape | solution.py:133
  265.2 0.3 convolution_reduce_fusion.1
  265.4 0.3 convolution_reduce_fusion
  265.7 0.6 fusion.5
  266.3 1.4 fusion
  267.7 0.6 pad_maximum_fusion.1
  (5 shorter events, 0.1 us)
Async XLA Ops:
  7.2 38.2 %copy-start.2 = (s32[128,2]{0,1:T(2,128)S(1)}, s32[128,2]{0,1:T(2,128)}, u32[]{:S(2)}) copy-start(s32[128,2]{0,1:T(2,128)} %param.9) | copy-start | bytes 3076
  7.2 189.4 %all-gather.3.cloned.1.call-start = ((), (), s32[]{:S(2)}) async-start(), calls=%async_computation.2 | async-start | bytes 12533760 | tf_op jit(solution)/shard_map/all_gather | solution.py:110
  8.5 35.9 %collective-permute-start = (bf16[144,2560]{1,0:T(8,128)(2,1)S(1)}, bf16[144,2560]{1,0:T(8,128)(2,1)S(1)}, u32[]{:S(2)}, u32[]{:S(2)}) collective-permute-start(bf16[144,2560]{1,0:T(8,128)(2,1)S(1)} %pad_maximum_fusion), channel_id=1, source_target_pairs={{0,260},{1,261},{2,294},{3,295},{4,320},{5,321},{6,354},{7,355},{8... | collective-permute-start | bytes 2211848 | tf_op jit(solution)/shard_map/ppermute | solution.py:109
  44.4 0.9 copy-start.1
  214.4 1.1 copy-start
  219.6 7.7 %copy-start.3 = (f32[128,2]{0,1:T(2,128)S(1)}, f32[128,2]{0,1:T(2,128)}, u32[]{:S(2)}) copy-start(f32[128,2]{0,1:T(2,128)} %param.10) | copy-start | bytes 3076
  219.6 42.7 %all-to-all-start.1 = ((bf16[32,9,2688]{2,1,0:T(8,128)(2,1)}), bf16[32,9,2688]{2,1,0:T(8,128)(2,1)}, u32[]{:S(2)}, u32[]{:S(2)}) async-start(bf16[32,9,2688]{2,1,0:T(8,128)(2,1)} %reshape.22), calls=%async_computation.1 | async-start | bytes 5505024 | tf_op jit(solution)/shard_map/all_to_all | solution.py:131
Sparse Core Ops, SparseCore 0:
  45.5 151.0 all-gather.2

commit v2 on v1

v2 whole, which is shorter than its diff:
```python
import jax
import jax.numpy as jnp
from jax import lax
from jax.experimental import pallas as pl
from jax.experimental.pallas import tpu as pltpu
from jax.sharding import Mesh, PartitionSpec as P

AXES = ("zl", "x", "y", "zh", "c")
PLANE = ("y", "x", "c")
RING = ("zh", "zl")
SIZES = (4, 4, 4, 4, 2)
EXPERTS = 32
LANES = 8
MAIN = EXPERTS * LANES
F32 = jnp.float32
BF16 = jnp.bfloat16

SHIFT = ((-6, 0, 0, 6), (-4, -2, 2, 4), (-2, -4, 4, 2), (0, -6, 6, 0))


def flat_index(zl, x, y, zh, c):
    return (((zl * 4 + x) * 4 + y) * 4 + zh) * 2 + c


def spread_pairs():
    pairs = []
    for zl in range(4):
        for x in range(4):
            for y in range(4):
                for zh in range(4):
                    for c in range(2):
                        z = (zh * 4 + zl + SHIFT[x][zl]) % 16
                        pairs.append(
                            (flat_index(zl, x, y, zh, c), flat_index(z % 4, zh, y, z // 4, c))
                        )
    return pairs


def dot(a, b):
    return jnp.dot(a, b, preferred_element_type=F32)


def dot_t(a, b):
    return lax.dot_general(a, b, (((1,), (1,)), ((), ())), preferred_element_type=F32)


def iota(shape, axis):
    return lax.broadcasted_iota(jnp.int32, shape, axis)


def split(value):
    high = value.astype(BF16).astype(F32)
    return high, value - high


def piece(i):
    return (384 * i, 384) if i < 4 else (1536 + 256 * (i - 4), 256)


def expert_kernel(rows_ref, slabs_ref, out_ref, weights, grads, sems):
    planes, height, width = slabs_ref.shape
    third = height // 3
    hid = planes * third

    def copy(plane, kind):
        return pltpu.make_async_copy(
            slabs_ref.at[plane, kind * third : (kind + 1) * third, :],
            weights.at[kind, plane * third : (plane + 1) * third, :],
            sems.at[kind, plane],
        )

    def arrive(kind):
        for plane in range(planes):
            copy(plane, kind).wait()

    for kind in (2, 0, 1):
        for plane in range(planes):
            copy(plane, kind).start()

    x = rows_ref[:, :width]
    arrive(2)
    q = dot_t(rows_ref[:, width:], weights[2])
    arrive(0)
    pre_gate = dot_t(x, weights[0])
    arrive(1)
    pre_up = dot_t(x, weights[1])
    sigma = jax.nn.sigmoid(pre_gate)
    act = pre_gate * sigma
    hidden = (act * pre_up).astype(BF16).astype(F32)
    grads[:, :hid] = (q * pre_up * sigma * (1.0 + pre_gate * (1.0 - sigma))).astype(BF16)
    grads[:, hid:] = (q * act).astype(BF16)
    term = jnp.sum(hidden * q, axis=1, keepdims=True)

    back = dot(grads[...], weights[0:2].reshape(2 * hid, width)).astype(BF16)
    out_ref[:, :width] = back[:MAIN]
    ninth = back[MAIN:]
    row, expert = iota((MAIN, EXPERTS), 0), iota((MAIN, EXPERTS), 1)
    two = jnp.zeros((MAIN, 256), F32)
    one = jnp.zeros((MAIN, 128), F32)
    for i in range(LANES):
        at, count = piece(i)
        got = dot((row == expert * LANES + i).astype(BF16), ninth[:, at : at + count])
        two = two + got[:, :256]
        if count == 384:
            one = one + got[:, 256:]
    high, low = split(term)
    lane, slot = iota((MAIN, 128), 1), iota((MAIN, 128), 0) % LANES
    kept = jnp.where(
        lane == slot, high[:MAIN], jnp.where(lane == slot + LANES, low[:MAIN], 0.0)
    ).astype(BF16)
    lane = iota((EXPERTS, 128), 1)
    last = jnp.where(
        lane == 16, high[MAIN:], jnp.where(lane == 17, low[MAIN:], 0.0)
    ).astype(BF16)
    to, come = iota((MAIN, MAIN), 0), iota((MAIN, MAIN), 1)
    gather = ((to % LANES == 4) & (to // LANES == come // LANES)).astype(BF16)
    one = one + dot(gather, kept) + dot((row == expert * LANES + 4).astype(BF16), last)
    out_ref[:, width : width + 256] = two.astype(BF16)
    out_ref[:, width + 256 :] = one.astype(BF16)


def expert_layer(rows, slabs):
    count, wide = rows.shape
    width = wide // 2
    planes, height, _ = slabs.shape
    hid = planes * height // 3
    return pl.pallas_call(
        expert_kernel,
        out_shape=jax.ShapeDtypeStruct((MAIN, width + 384), BF16),
        in_specs=[
            pl.BlockSpec(memory_space=pltpu.VMEM),
            pl.BlockSpec(memory_space=pl.ANY),
        ],
        out_specs=pl.BlockSpec(memory_space=pltpu.VMEM),
        scratch_shapes=[
            pltpu.VMEM((3, hid, width), BF16),
            pltpu.VMEM((count, 2 * hid), BF16),
            pltpu.SemaphoreType.DMA((3, planes)),
        ],
        compiler_params=pltpu.CompilerParams(vmem_limit_bytes=56 * 1024 * 1024),
    )(rows, slabs)


def home_kernel(home_ref, base_ref, slot_ref, gates_ref, grad_ref, term_ref):
    tok_rows, width = grad_ref.shape
    base, slot, gates = base_ref[...], slot_ref[...], gates_ref[...]
    col = iota((tok_rows, MAIN), 1)

    def weights(at):
        total = jnp.zeros((tok_rows, MAIN), F32)
        for k in range(2):
            total = total + jnp.where(col == at[:, k : k + 1], gates[:, k : k + 1], 0.0)
        return jnp.concatenate([part.astype(BF16) for part in split(total)], axis=0)

    def both(got):
        return got[:tok_rows] + got[tok_rows:]

    main = weights(jnp.where(slot < LANES, base + slot, -1))
    ninth_at = jnp.where(slot < LANES, -1000, base)
    for i in range(LANES):
        at, count = piece(i)
        got = dot(main, home_ref[:, at : at + count])
        got = got + dot(weights(ninth_at + i), home_ref[:, width : width + count])
        grad_ref[:, at : at + count] = both(got).astype(BF16)
    lane = iota((tok_rows, 128), 1)
    terms = []
    for k in range(2):
        got = dot((col == base[:, k : k + 1] + 4).astype(BF16), home_ref[:, width + 256 :])
        mine = slot[:, k : k + 1]
        low = jnp.where(mine < LANES, mine + LANES, 17)
        high = jnp.where(mine < LANES, mine, 16)
        terms.append(jnp.sum(jnp.where((lane == high) | (lane == low), got, 0.0), axis=1, keepdims=True))
    term_ref[...] = jnp.where(iota((tok_rows, 2), 1) == 0, terms[0], terms[1])


def bring_home(home, base, slot, gates, width):
    tok_rows = base.shape[0]
    return pl.pallas_call(
        home_kernel,
        out_shape=(
            jax.ShapeDtypeStruct((tok_rows, width), BF16),
            jax.ShapeDtypeStruct((tok_rows, 2), F32),
        ),
        in_specs=[pl.BlockSpec(memory_space=pltpu.VMEM)] * 4,
        out_specs=[pl.BlockSpec(memory_space=pltpu.VMEM)] * 2,
        compiler_params=pltpu.CompilerParams(vmem_limit_bytes=32 * 1024 * 1024),
    )(home, base, slot, gates)


def exchange(wire):
    sent = wire.reshape(EXPERTS, LANES, wire.shape[1])
    got = lax.all_to_all(sent, PLANE, split_axis=0, concat_axis=0, tiled=True)
    return got.reshape(wire.shape)


def local(tokens, cotangent, expert_ids, gate_values, w_gate, w_up, w_down):
    tok_rows, width = tokens.shape

    slab = jnp.concatenate([w_gate[0], w_up[0], w_down[0]], axis=0)
    slab = lax.ppermute(slab, AXES, spread_pairs())
    slabs = lax.all_gather(slab, RING, axis=0, tiled=False)

    names = jnp.arange(EXPERTS, dtype=jnp.int32)
    pick = (expert_ids[:, :, None] == names[None, None, :]).astype(F32)
    member = jnp.sum(pick, axis=1)
    row = jnp.arange(tok_rows, dtype=jnp.int32)
    earlier = (row[None, :] < row[:, None]).astype(BF16)
    before = dot(earlier, member.astype(BF16))
    slot = jnp.sum(before[:, None, :] * pick, axis=2).astype(jnp.int32)
    base = expert_ids * LANES

    spots = jnp.arange(MAIN, dtype=jnp.int32)[:, None]
    main_at = jnp.where(slot < LANES, base + slot, -1)
    ninth_at = jnp.where(slot < LANES, -1, expert_ids)
    main_pick = ((spots == main_at[None, :, 0]) | (spots == main_at[None, :, 1])).astype(BF16)
    heads = names[:, None]
    ninth_pick = ((heads == ninth_at[None, :, 0]) | (heads == ninth_at[None, :, 1])).astype(BF16)
    both = jnp.concatenate([tokens, cotangent], axis=1)
    main = dot(main_pick, both).astype(BF16)
    ninth = dot(ninth_pick, both).astype(BF16).reshape(MAIN, 2 * width // LANES)
    wire = exchange(jnp.concatenate([main, ninth], axis=1))
    rows = jnp.concatenate(
        [wire[:, : 2 * width], wire[:, 2 * width :].reshape(EXPERTS, 2 * width)], axis=0
    )

    home = exchange(expert_layer(rows, slabs))
    return bring_home(home, base, slot, gate_values, width)


def solution(mesh):
    fine = Mesh(mesh.devices.reshape(SIZES), AXES)
    rows = P(AXES, None)
    weights = P(("y", "zh", "c"), ("zl", "x"), None)
    return jax.shard_map(
        local,
        mesh=fine,
        in_specs=(rows, rows, rows, rows, weights, weights, weights),
        out_specs=(rows, rows),
        check_vma=False,
    )
```

time: 276 us -> 249 us (0.902)
  blocking collectives: 78.2 us -> 53.1 us
  waiting for transfers between devices: 119 us -> 133 us
  local copies, waits for them, and re-layouts: 16.2 us -> 3.44 us
  matrix products: 4.88 us -> 1.26 us
  other arithmetic: 1.85 us -> 4.82 us
    all_gather x1, waiting for transfers between devices: 63.3 us -> 91.5 us  [local(): slabs = lax.all_gather(slab, RING, axis=0, tiled=False)]
    all_to_all x1, blocking collectives: 78.2 us -> 53.1 us  [exchange(): got = lax.all_to_all(sent, PLANE, split_axis=0, concat_axis=0, tiled=True)]
    reshape x4 -> x1, local copies, waits for them, and re-layouts: 14.1 us -> 0.15 us  [local(): wire[:, 2 * width:].reshape(EXPERTS, 2 * width)]
    all_to_all x1, waiting for transfers between devices: 35 us -> 21.3 us  [exchange(): got = lax.all_to_all(sent, PLANE, split_axis=0, concat_axis=0, tiled=True)]
    dot_general x6 -> x3, matrix products: 4.88 us -> 1.26 us  [dot(): return jnp.dot(a, b, preferred_element_type=F32)]
    pallas_call x1 -> x2, Pallas kernels: 17.8 us -> 15.5 us  [the longest x1 13.6 us: expert_layer(): pl.pallas_call(expert_kernel, out_shape=jax.ShapeDtypeStruct((MAIN, width...]
  transfers between devices with their start and end apart: 3 -> 3, of which waited for: 3 -> 3; matrix products, arithmetic and copies ran while one was open for 4% -> 3% of each run, Pallas kernels for 0% -> 0%
where the time goes in v2:
time: 249 us
  waiting for transfers between devices  133 us (53%)
  blocking collectives  53.1 us (21%)
  starting transfers between devices  23 us (9%)
  Pallas kernels  15.5 us (6%)
  between operations  14.2 us (6%)
  other arithmetic  4.82 us (2%)
  local copies, waits for them, and re-layouts  3.44 us (1%)
    all_gather x1, waiting for transfers between devices, local(): slabs = lax.all_gather(slab, RING, axis=0, tiled=False)  91.5 us
    all_to_all x1, blocking collectives, exchange(): got = lax.all_to_all(sent, PLANE, split_axis=0, concat_axis=0, tiled=True)  53.1 us
    all_to_all x1, waiting for transfers between devices, exchange(): got = lax.all_to_all(sent, PLANE, split_axis=0, concat_axis=0, tiled=True)  21.3 us
    ppermute x1, waiting for transfers between devices, local(): slab = lax.ppermute(slab, AXES, spread_pairs())  20.6 us
    ppermute x1, starting transfers between devices, local(): slab = lax.ppermute(slab, AXES, spread_pairs())  15.4 us
    pallas_call x1, Pallas kernels, expert_layer(): pl.pallas_call(expert_kernel, out_shape=jax.ShapeDtypeStruct((MAIN, width...  13.6 us
    all_to_all x1, starting transfers between devices, exchange(): got = lax.all_to_all(sent, PLANE, split_axis=0, concat_axis=0, tiled=True)  7.54 us
  transfers between devices with their start and end apart: 3, of which 3 were waited for; matrix products, arithmetic and copies ran while one was open for 3% of the time, Pallas kernels for 0%

profile of v2, /device:TPU:1, one launch (start us, length us, event | category | flops | bytes accessed | tf_op | source)
XLA Modules:
  0.0 248.6 jit_solution(10393998069633374585)
XLA Ops:
  7.2 0.0 copy-start.1
  7.2 0.0 all-gather.3.cloned.1.call-start
  7.2 1.3 pad_maximum_fusion.2
  8.6 15.4 %collective-permute-start = (bf16[144,2560]{1,0:T(8,128)(2,1)S(1)}, bf16[144,2560]{1,0:T(8,128)(2,1)S(1)}, u32[]{:S(2)}, u32[]{:S(2)}) collective-permute-start(bf16[144,2560]{1,0:T(8,128)(2,1)S(1)} %pad_maximum_fusion.2), channel_id=1, source_target_pairs={{0,260},{1,261},{2,294},{3,295},{4,320},{5,321},{6,354},{7,355},{8... | collective-permute-start | bytes 2211848 | tf_op jit(solution)/shard_map/ppermute | solution.py:200
  23.9 20.6 %collective-permute-done = bf16[144,2560]{1,0:T(8,128)(2,1)S(1)} collective-permute-done((bf16[144,2560]{1,0:T(8,128)(2,1)S(1)}, bf16[144,2560]{1,0:T(8,128)(2,1)S(1)}, u32[]{:S(2)}, u32[]{:S(2)}) %collective-permute-start) | collective-permute-done | bytes 737312 | tf_op jit(solution)/shard_map/ppermute | solution.py:200
  44.5 0.9 copy-done
  45.4 0.0 all-gather.3.cloned.1.call-update
  45.4 0.8 copy.22
  46.2 0.7 convert_reduce_fusion
  46.9 0.1 fusion.5
  47.0 0.7 select_reduce_fusion
  47.7 0.1 copy.21
  47.9 0.2 slice_reduce_fusion.1
  48.1 0.0 copy-done.1
  48.1 0.1 constant_dynamic-update-slice_fusion.1
  48.2 0.0 copy-done.2
  48.2 0.1 constant_dynamic-update-slice_fusion
  48.3 0.3 convolution_convert_fusion.1
  48.6 0.8 fusion
  49.4 0.2 pad_maximum_fusion
  49.6 53.1 %all_to_all.10 = bf16[32,8,5760]{2,1,0:T(8,128)(2,1)S(1)} all-to-all(bf16[32,8,5760]{2,1,0:T(8,128)(2,1)S(1)} %pad_maximum_fusion), channel_id=1, replica_groups=mesh['zl'=4,'x'=4,'y'=4,'zh'=4,'c'=2] {'y','x','c'}, dimensions={0} | all-to-all | bytes 5898240 | tf_op jit(solution)/shard_map/all_to_all | solution.py:192
  102.8 0.3 slice.28
  103.1 0.2 reshape.28
  103.3 1.9 pad_maximum_fusion.1.rows_ref
  105.2 91.5 %all-gather.3.cloned.1.call-done = bf16[2304,2560]{1,0:T(8,128)(2,1)} async-done(((bf16[144,2560]{1,0:T(8,128)(2,1)}), bf16[2304,2560]{1,0:T(8,128)(2,1)}) %all-gather.3.cloned.1.call-update) | async-done | bytes 11796496 | tf_op jit(solution)/shard_map/all_gather | solution.py:201
  196.6 13.6 %shard_map.86 = bf16[256,2944]{1,0:T(8,128)(2,1)} custom-call(bf16[288,5120]{1,0:T(8,128)(2,1)} %pad_maximum_fusion.1.rows_ref, bf16[16,144,2560]{2,1,0:T(8,128)(2,1)} %bitcast.15), custom_call_target="tpu_custom_call" | custom-call | tf_op jit(solution)/shard_map/pallas_call | solution.py:127
  210.2 0.0 copy-start.3
  210.2 7.5 %all-to-all-start.1 = ((bf16[32,8,2944]{2,1,0:T(8,128)(2,1)}), bf16[32,8,2944]{2,1,0:T(8,128)(2,1)S(1)}, u32[]{:S(2)}, u32[]{:S(2)}) async-start(bf16[32,8,2944]{2,1,0:T(8,128)(2,1)} %bitcast.18), calls=%async_computation.1 | async-start | bytes 3014656 | tf_op jit(solution)/shard_map/all_to_all | solution.py:192
  217.8 0.1 copy.24.gates_ref
  217.9 21.3 %all-to-all-done.1 = bf16[32,8,2944]{2,1,0:T(8,128)(2,1)S(1)} async-done(((bf16[32,8,2944]{2,1,0:T(8,128)(2,1)}), bf16[32,8,2944]{2,1,0:T(8,128)(2,1)S(1)}, u32[]{:S(2)}, u32[]{:S(2)}) %all-to-all-start.1) | async-done | bytes 1507360 | tf_op jit(solution)/shard_map/all_to_all | solution.py:192
  239.2 2.0 shard_map.87
  241.2 0.6 copy.25
  (7 shorter events, 0.1 us)
Async XLA Ops:
  7.2 40.9 %copy-start.1 = (bf16[128,2560]{1,0:T(8,128)(2,1)S(1)}, bf16[128,2560]{1,0:T(8,128)(2,1)}, u32[]{:S(2)}) copy-start(bf16[128,2560]{1,0:T(8,128)(2,1)} %param.7) | copy-start | bytes 1966084
  7.2 41.0 %copy-start.2 = (bf16[128,2560]{1,0:T(8,128)(2,1)S(1)}, bf16[128,2560]{1,0:T(8,128)(2,1)}, u32[]{:S(2)}) copy-start(bf16[128,2560]{1,0:T(8,128)(2,1)} %param.8) | copy-start | bytes 1966084
  7.2 189.4 %all-gather.3.cloned.1.call-start = ((), (), s32[]{:S(2)}) async-start(), calls=%async_computation.2 | async-start | bytes 12533760 | tf_op jit(solution)/shard_map/all_gather | solution.py:201
  8.6 35.9 %collective-permute-start = (bf16[144,2560]{1,0:T(8,128)(2,1)S(1)}, bf16[144,2560]{1,0:T(8,128)(2,1)S(1)}, u32[]{:S(2)}, u32[]{:S(2)}) collective-permute-start(bf16[144,2560]{1,0:T(8,128)(2,1)S(1)} %pad_maximum_fusion.2), channel_id=1, source_target_pairs={{0,260},{1,261},{2,294},{3,295},{4,320},{5,321},{6,354},{7,355},{8... | collective-permute-start | bytes 2211848 | tf_op jit(solution)/shard_map/ppermute | solution.py:200
  44.5 0.9 copy-start
  210.2 7.6 %copy-start.3 = (f32[128,2]{0,1:T(2,128)S(1)}, f32[128,2]{0,1:T(2,128)}, u32[]{:S(2)}) copy-start(f32[128,2]{0,1:T(2,128)} %param.10) | copy-start | bytes 3076
  210.2 29.0 %all-to-all-start.1 = ((bf16[32,8,2944]{2,1,0:T(8,128)(2,1)}), bf16[32,8,2944]{2,1,0:T(8,128)(2,1)S(1)}, u32[]{:S(2)}, u32[]{:S(2)}) async-start(bf16[32,8,2944]{2,1,0:T(8,128)(2,1)} %bitcast.18), calls=%async_computation.1 | async-start | bytes 3014656 | tf_op jit(solution)/shard_map/all_to_all | solution.py:192
Sparse Core Ops, SparseCore 0:
  45.5 151.0 all-gather.2

commit v3 on v2

--- a/solution.py
+++ b/solution.py
@@ -1,3 +1,5 @@
+import functools
+
 import jax
 import jax.numpy as jnp
 from jax import lax
@@ -12,6 +14,8 @@
 EXPERTS = 32
 LANES = 8
 MAIN = EXPERTS * LANES
+VMEM_BYTES = 56 * 1024 * 1024
+PARTS = ((0, 16),)
 F32 = jnp.float32
 BF16 = jnp.bfloat16
 
@@ -36,6 +40,20 @@
     return pairs
 
 
+def ring_pairs(step):
+    pairs = []
+    for zl in range(4):
+        for x in range(4):
+            for y in range(4):
+                for zh in range(4):
+                    for c in range(2):
+                        z = (zh * 4 + zl + step) % 16
+                        pairs.append(
+                            (flat_index(zl, x, y, zh, c), flat_index(z % 4, x, y, z // 4, c))
+                        )
+    return pairs
+
+
 def dot(a, b):
     return jnp.dot(a, b, preferred_element_type=F32)
 
@@ -57,43 +75,10 @@
     return (384 * i, 384) if i < 4 else (1536 + 256 * (i - 4), 256)
 
 
-def expert_kernel(rows_ref, slabs_ref, out_ref, weights, grads, sems):
-    planes, height, width = slabs_ref.shape
-    third = height // 3
-    hid = planes * third
-
-    def copy(plane, kind):
-        return pltpu.make_async_copy(
-            slabs_ref.at[plane, kind * third : (kind + 1) * third, :],
-            weights.at[kind, plane * third : (plane + 1) * third, :],
-            sems.at[kind, plane],
-        )
-
-    def arrive(kind):
-        for plane in range(planes):
-            copy(plane, kind).wait()
-
-    for kind in (2, 0, 1):
-        for plane in range(planes):
-            copy(plane, kind).start()
-
-    x = rows_ref[:, :width]
-    arrive(2)
-    q = dot_t(rows_ref[:, width:], weights[2])
-    arrive(0)
-    pre_gate = dot_t(x, weights[0])
-    arrive(1)
-    pre_up = dot_t(x, weights[1])
-    sigma = jax.nn.sigmoid(pre_gate)
-    act = pre_gate * sigma
-    hidden = (act * pre_up).astype(BF16).astype(F32)
-    grads[:, :hid] = (q * pre_up * sigma * (1.0 + pre_gate * (1.0 - sigma))).astype(BF16)
-    grads[:, hid:] = (q * act).astype(BF16)
-    term = jnp.sum(hidden * q, axis=1, keepdims=True)
-
-    back = dot(grads[...], weights[0:2].reshape(2 * hid, width)).astype(BF16)
+def back_wire(back, term, out_ref):
+    width = back.shape[1]
+    ninth = back[MAIN:]
     out_ref[:, :width] = back[:MAIN]
-    ninth = back[MAIN:]
     row, expert = iota((MAIN, EXPERTS), 0), iota((MAIN, EXPERTS), 1)
     two = jnp.zeros((MAIN, 256), F32)
     one = jnp.zeros((MAIN, 128), F32)
@@ -119,26 +104,119 @@
     out_ref[:, width + 256 :] = one.astype(BF16)
 
 
-def expert_layer(rows, slabs):
-    count, wide = rows.shape
-    width = wide // 2
-    planes, height, _ = slabs.shape
-    hid = planes * height // 3
+def take_rows(x_wire, dy_wire, x, dy):
+    width = x.shape[1]
+    part = width // 4
+    x[:MAIN, :] = x_wire[:, :width]
+    dy[:MAIN, :] = dy_wire[:, :width]
+    sender, row = iota((EXPERTS, MAIN), 0), iota((EXPERTS, MAIN), 1)
+    for i in range(LANES):
+        hot = (row == sender * LANES + i).astype(BF16)
+        ref, at = (x, i * part) if i < 4 else (dy, (i - 4) * part)
+        ref[MAIN:, at : at + 384] = dot(hot, x_wire[:, width:]).astype(BF16)
+        ref[MAIN:, at + 384 : at + part] = dot(hot, dy_wire[:, width:]).astype(BF16)
+
+
+def expert_kernel(count, first, last, *refs):
+    refs = list(refs)
+    x_wire, dy_wire = refs.pop(0), refs.pop(0)
+    slices = [(refs.pop(0), refs.pop(0)) for _ in range(count)]
+    if not first:
+        total_in, term_in = refs.pop(0), refs.pop(0)
+    if last:
+        out_ref = refs.pop(0)
+    else:
+        total_out, term_out = refs.pop(0), refs.pop(0)
+    weights, grads, x, dy, sems = refs[:5]
+    height, half = slices[0][0].shape
+    third = height // 3
+    hid, width = count * third, 2 * half
+
+    def copies(kind):
+        return [
+            pltpu.make_async_copy(
+                slices[n][h].at[kind * third : (kind + 1) * third, :],
+                weights.at[kind, n * third : (n + 1) * third, h * half : (h + 1) * half],
+                sems.at[kind, n, h],
+            )
+            for n in range(count)
+            for h in range(2)
+        ]
+
+    def arrive(kind):
+        for copy in copies(kind):
+            copy.wait()
+
+    for kind in (2, 0, 1):
+        for copy in copies(kind):
+            copy.start()
+    if not first:
+        held, held_sem = refs[5:]
+        fetch = pltpu.make_async_copy(total_in, held, held_sem)
+        fetch.start()
+
+    take_rows(x_wire, dy_wire, x, dy)
+    arrive(2)
+    q = dot_t(dy[...], weights[2])
+    arrive(0)
+    pre_gate = dot_t(x[...], weights[0])
+    arrive(1)
+    pre_up = dot_t(x[...], weights[1])
+    sigma = jax.nn.sigmoid(pre_gate)
+    act = pre_gate * sigma
+    hidden = (act * pre_up).astype(BF16).astype(F32)
+    grads[:, :hid] = (q * pre_up * sigma * (1.0 + pre_gate * (1.0 - sigma))).astype(BF16)
+    grads[:, hid:] = (q * act).astype(BF16)
+    term = jnp.sum(hidden * q, axis=1, keepdims=True)
+    back = dot(grads[...], weights[0:2].reshape(2 * hid, width))
+    if not first:
+        fetch.wait()
+        back = back + held[...]
+        term = term + term_in[...]
+    if last:
+        back_wire(back.astype(BF16), term, out_ref)
+    else:
+        total_out[...] = back
+        term_out[...] = term
+
+
+def expert_part(wires, slices, before, last):
+    places, width = MAIN + EXPERTS, 2 * slices[0][0].shape[1]
+    count = len(slices)
+    hid = count * slices[0][0].shape[0] // 3
+    first = before is None
+    vmem, hbm = pl.BlockSpec(memory_space=pltpu.VMEM), pl.BlockSpec(memory_space=pl.ANY)
+    if last:
+        out_shape = jax.ShapeDtypeStruct((MAIN, width + 384), BF16)
+        out_specs = vmem
+    else:
+        out_shape = (
+            jax.ShapeDtypeStruct((places, width), F32),
+            jax.ShapeDtypeStruct((places, 1), F32),
+        )
+        out_specs = (vmem, vmem)
+    scratch = [
+        pltpu.VMEM((3, hid, width), BF16),
+        pltpu.VMEM((places, 2 * hid), BF16),
+        pltpu.VMEM((places, width), BF16),
+        pltpu.VMEM((places, width), BF16),
+        pltpu.SemaphoreType.DMA((3, count, 2)),
+    ]
+    if not first:
+        scratch += [pltpu.VMEM((places, width), F32), pltpu.SemaphoreType.DMA]
+    operands = list(wires) + [half for pair in slices for half in pair]
+    in_specs = [vmem] * 2 + [hbm] * (2 * count)
+    if not first:
+        operands += list(before)
+        in_specs += [hbm, vmem]
     return pl.pallas_call(
-        expert_kernel,
-        out_shape=jax.ShapeDtypeStruct((MAIN, width + 384), BF16),
-        in_specs=[
-            pl.BlockSpec(memory_space=pltpu.VMEM),
-            pl.BlockSpec(memory_space=pl.ANY),
-        ],
-        out_specs=pl.BlockSpec(memory_space=pltpu.VMEM),
-        scratch_shapes=[
-            pltpu.VMEM((3, hid, width), BF16),
-            pltpu.VMEM((count, 2 * hid), BF16),
-            pltpu.SemaphoreType.DMA((3, planes)),
-        ],
-        compiler_params=pltpu.CompilerParams(vmem_limit_bytes=56 * 1024 * 1024),
-    )(rows, slabs)
+        functools.partial(expert_kernel, count, first, last),
+        out_shape=out_shape,
+        in_specs=in_specs,
+        out_specs=out_specs,
+        scratch_shapes=scratch,
+        compiler_params=pltpu.CompilerParams(vmem_limit_bytes=VMEM_BYTES),
+    )(*operands)
 
 
 def home_kernel(home_ref, base_ref, slot_ref, gates_ref, grad_ref, term_ref):
@@ -187,6 +265,55 @@
     )(home, base, slot, gates)
 
 
+def send_kernel(tokens_ref, cotangent_ref, ids_ref, x_ref, dy_ref, base_ref, slot_ref):
+    tok_rows, width = tokens_ref.shape
+    ids = ids_ref[...]
+    lane = iota((tok_rows, 128), 1)
+    picks = [(lane == ids[:, k : k + 1]).astype(F32) for k in range(2)]
+    earlier = (iota((tok_rows, tok_rows), 1) < iota((tok_rows, tok_rows), 0)).astype(BF16)
+    before = dot(earlier, (picks[0] + picks[1]).astype(BF16))
+    slots = [jnp.sum(before * pick, axis=1, keepdims=True).astype(jnp.int32) for pick in picks]
+    slot = jnp.where(iota((tok_rows, 2), 1) == 0, slots[0], slots[1])
+    base = ids * LANES
+    base_ref[...] = base
+    slot_ref[...] = slot
+    col = iota((tok_rows, MAIN), 1)
+    main_at = jnp.where(slot < LANES, base + slot, -1)
+    ninth_at = jnp.where(slot < LANES, -1, ids)
+    main = ((col == main_at[:, 0:1]) | (col == main_at[:, 1:2])).astype(F32).T.astype(BF16)
+    ninth = ((lane == ninth_at[:, 0:1]) | (lane == ninth_at[:, 1:2])).astype(F32).T[:EXPERTS]
+    ninth = ninth.astype(BF16)
+    row, expert = iota((MAIN, EXPERTS), 0), iota((MAIN, EXPERTS), 1)
+    part = width // 4
+    beside = jnp.zeros((MAIN, part), F32)
+    for which, ref in enumerate((tokens_ref, cotangent_ref)):
+        last = dot(ninth, ref[...]).astype(BF16)
+        for i in range(4):
+            hot = (row == expert * LANES + 4 * which + i).astype(BF16)
+            beside = beside + dot(hot, last[:, i * part : (i + 1) * part])
+    x_ref[:, :width] = dot(main, tokens_ref[...]).astype(BF16)
+    dy_ref[:, :width] = dot(main, cotangent_ref[...]).astype(BF16)
+    x_ref[:, width:] = beside[:, :384].astype(BF16)
+    dy_ref[:, width:] = beside[:, 384:].astype(BF16)
+
+
+def send_rows(tokens, cotangent, expert_ids):
+    tok_rows, width = tokens.shape
+    vmem = pl.BlockSpec(memory_space=pltpu.VMEM)
+    return pl.pallas_call(
+        send_kernel,
+        out_shape=(
+            jax.ShapeDtypeStruct((MAIN, width + 384), BF16),
+            jax.ShapeDtypeStruct((MAIN, width + 256), BF16),
+            jax.ShapeDtypeStruct((tok_rows, 2), jnp.int32),
+            jax.ShapeDtypeStruct((tok_rows, 2), jnp.int32),
+        ),
+        in_specs=[vmem] * 3,
+        out_specs=[vmem] * 4,
+        compiler_params=pltpu.CompilerParams(vmem_limit_bytes=VMEM_BYTES),
+    )(tokens, cotangent, expert_ids)
+
+
 def exchange(wire):
     sent = wire.reshape(EXPERTS, LANES, wire.shape[1])
     got = lax.all_to_all(sent, PLANE, split_axis=0, concat_axis=0, tiled=True)
@@ -197,34 +324,24 @@
     tok_rows, width = tokens.shape
 
     slab = jnp.concatenate([w_gate[0], w_up[0], w_down[0]], axis=0)
-    slab = lax.ppermute(slab, AXES, spread_pairs())
-    slabs = lax.all_gather(slab, RING, axis=0, tiled=False)
-
-    names = jnp.arange(EXPERTS, dtype=jnp.int32)
-    pick = (expert_ids[:, :, None] == names[None, None, :]).astype(F32)
-    member = jnp.sum(pick, axis=1)
-    row = jnp.arange(tok_rows, dtype=jnp.int32)
-    earlier = (row[None, :] < row[:, None]).astype(BF16)
-    before = dot(earlier, member.astype(BF16))
-    slot = jnp.sum(before[:, None, :] * pick, axis=2).astype(jnp.int32)
-    base = expert_ids * LANES
-
-    spots = jnp.arange(MAIN, dtype=jnp.int32)[:, None]
-    main_at = jnp.where(slot < LANES, base + slot, -1)
-    ninth_at = jnp.where(slot < LANES, -1, expert_ids)
-    main_pick = ((spots == main_at[None, :, 0]) | (spots == main_at[None, :, 1])).astype(BF16)
-    heads = names[:, None]
-    ninth_pick = ((heads == ninth_at[None, :, 0]) | (heads == ninth_at[None, :, 1])).astype(BF16)
-    both = jnp.concatenate([tokens, cotangent], axis=1)
-    main = dot(main_pick, both).astype(BF16)
-    ninth = dot(ninth_pick, both).astype(BF16).reshape(MAIN, 2 * width // LANES)
-    wire = exchange(jnp.concatenate([main, ninth], axis=1))
-    rows = jnp.concatenate(
-        [wire[:, : 2 * width], wire[:, 2 * width :].reshape(EXPERTS, 2 * width)], axis=0
-    )
-
-    home = exchange(expert_layer(rows, slabs))
-    return bring_home(home, base, slot, gate_values, width)
+    spread, up, down = spread_pairs(), ring_pairs(1), ring_pairs(-1)
+    half = width // 2
+    right = [lax.ppermute(part, AXES, spread) for part in (slab[:, :half], slab[:, half:])]
+    x_wire, dy_wire, base, slot = send_rows(tokens, cotangent, expert_ids)
+    dy_wire, right[0] = lax.optimization_barrier((dy_wire, right[0]))
+    left = right
+    slices = [right]
+    for _ in range(7):
+        right = [lax.ppermute(part, AXES, up) for part in right]
+        left = [lax.ppermute(part, AXES, down) for part in left]
+        slices += [right, left]
+    slices.append([lax.ppermute(right[0], AXES, up), lax.ppermute(left[1], AXES, down)])
+
+    wires = exchange(x_wire), exchange(dy_wire)
+    total = None
+    for begin, end in PARTS:
+        total = expert_part(wires, slices[begin:end], total, end == len(slices))
+    return bring_home(exchange(total), base, slot, gate_values, width)
 
 
 def solution(mesh):

time: 249 us -> 234 us (0.940)
  starting transfers between devices: 23 us -> 157 us
  waiting for transfers between devices: 133 us -> 51.2 us
  blocking collectives: 53.1 us -> 0 us
  between operations: 14.2 us -> 1.35 us
  Pallas kernels: 15.5 us -> 20.7 us
  other arithmetic: 4.82 us -> 1.23 us
    ppermute x1 -> x32, starting transfers between devices: 15.4 us -> 126 us  [the longest x14 72.4 us: local(): left = [lax.ppermute(part, AXES, down) for part in left]]
    all_gather x1 -> x0, waiting for transfers between devices: 91.5 us -> none  [local(): slabs = lax.all_gather(slab, RING, axis=0, tiled=False)]
    all_to_all x1 -> x0, blocking collectives: 53.1 us -> none  [exchange(): got = lax.all_to_all(sent, PLANE, split_axis=0, concat_axis=0, tiled=True)]
    all_to_all x1 -> x3, starting transfers between devices: 7.54 us -> 30.9 us  [exchange(): got = lax.all_to_all(sent, PLANE, split_axis=0, concat_axis=0, tiled=True)]
    ppermute x1 -> x32, waiting for transfers between devices: 20.6 us -> 29.9 us  [the longest x14 12.6 us: local(): right = [lax.ppermute(part, AXES, up) for part in right]]
    pallas_call x1 -> x2, Pallas kernels: 13.6 us -> 18.7 us  [the longest x1 14 us: expert_part(): pl.pallas_call(functools.partial(expert_kernel, count, first, last), out_...]
    all_to_all x1 -> x3, waiting for transfers between devices: 21.3 us -> 21.3 us  [exchange(): got = lax.all_to_all(sent, PLANE, split_axis=0, concat_axis=0, tiled=True)]
  transfers between devices with their start and end apart: 3 -> 35, of which waited for: 3 -> 15; matrix products, arithmetic and copies ran while one was open for 3% -> 0% of each run, Pallas kernels for 0% -> 2%
where the time goes in v3:
time: 234 us; the launch traced here: 233 us
  starting transfers between devices  157 us (67%)
  waiting for transfers between devices  51.2 us (22%)
  Pallas kernels  20.7 us (9%)
    ppermute x14, starting transfers between devices, local(): left = [lax.ppermute(part, AXES, down) for part in left]  72.4 us
    all_to_all x3, starting transfers between devices, exchange(): got = lax.all_to_all(sent, PLANE, split_axis=0, concat_axis=0, tiled=True)  30.9 us
    ppermute x14, starting transfers between devices, local(): right = [lax.ppermute(part, AXES, up) for part in right]  26.8 us
    all_to_all x3, waiting for transfers between devices, exchange(): got = lax.all_to_all(sent, PLANE, split_axis=0, concat_axis=0, tiled=True)  21.3 us
    ppermute x2, starting transfers between devices, local(): lax.ppermute(part, AXES, spread)  20 us
    pallas_call x1, Pallas kernels, expert_part(): pl.pallas_call(functools.partial(expert_kernel, count, first, last), out_...  14 us
    ppermute x14, waiting for transfers between devices, local(): right = [lax.ppermute(part, AXES, up) for part in right]  12.6 us
    ppermute x2, waiting for transfers between devices, local(): lax.ppermute(part, AXES, spread)  8.49 us
  transfers between devices with their start and end apart: 35, of which 15 were waited for; matrix products, arithmetic and copies ran while one was open for 0% of the time, Pallas kernels for 2%

profile of v3, /device:TPU:1, one launch (start us, length us, event | category | flops | bytes accessed | tf_op | source)
XLA Modules:
  0.0 232.9 jit_solution(10852655811632990823)
XLA Ops:
  1.9 15.4 %collective-permute-start = (bf16[144,1280]{1,0:T(8,128)(2,1)S(1)}, bf16[144,1280]{1,0:T(8,128)(2,1)S(1)}, u32[]{:S(2)}, u32[]{:S(2)}) collective-permute-start(bf16[144,1280]{1,0:T(8,128)(2,1)S(1)} %get-tuple-element.17), channel_id=1, source_target_pairs={{0,260},{1,261},{2,294},{3,295},{4,320},{5,321},{6,354},{7,355},{8... | collective-permute-start | bytes 1105928 | tf_op jit(solution)/shard_map/ppermute | solution.py:329
  17.3 4.7 %collective-permute-start.1 = (bf16[144,1280]{1,0:T(8,128)(2,1)S(1)}, bf16[144,1280]{1,0:T(8,128)(2,1)S(1)}, u32[]{:S(2)}, u32[]{:S(2)}) collective-permute-start(bf16[144,1280]{1,0:T(8,128)(2,1)S(1)} %get-tuple-element.16), channel_id=1, source_target_pairs={{0,260},{1,261},{2,294},{3,295},{4,320},{5,321},{6,354},{7,355},{8... | collective-permute-start | bytes 1105928 | tf_op jit(solution)/shard_map/ppermute | solution.py:329
  22.7 4.7 %shard_map.86 = (bf16[256,2944]{1,0:T(8,128)(2,1)}, bf16[256,2816]{1,0:T(8,128)(2,1)}, s32[128,2]{1,0:T(8,128)}, s32[128,2]{1,0:T(8,128)}) custom-call(bf16[128,2560]{1,0:T(8,128)(2,1)} %tokens_ref.1, bf16[128,2560]{1,0:T(8,128)(2,1)} %cotangent_ref.1, s32[128,2]{1,0:T(8,128)} %copy.9.ids_ref), custom_call_target="tpu_custom_call" | custom-call | tf_op jit(solution)/shard_map/pallas_call | solution.py:303
  27.5 1.9 collective-permute-start.2
  29.4 8.5 %collective-permute-done.1.refs_3_ = bf16[144,1280]{1,0:T(8,128)(2,1)S(1)} collective-permute-done((bf16[144,1280]{1,0:T(8,128)(2,1)S(1)}, bf16[144,1280]{1,0:T(8,128)(2,1)S(1)}, u32[]{:S(2)}, u32[]{:S(2)}) %collective-permute-start.1) | collective-permute-done | bytes 368672 | tf_op jit(solution)/shard_map/ppermute | solution.py:329
  37.9 12.9 %collective-permute-start.5 = (bf16[144,1280]{1,0:T(8,128)(2,1)S(1)}, bf16[144,1280]{1,0:T(8,128)(2,1)S(1)}, u32[]{:S(2)}, u32[]{:S(2)}) collective-permute-start(bf16[144,1280]{1,0:T(8,128)(2,1)S(1)} %collective-permute-done.1.refs_3_), channel_id=1, source_target_pairs={{0,390},{1,391},{2,384},{3,385},{4,386},{5,387},{6,388},{7,389},{8... | collective-permute-start | bytes 1105928 | tf_op jit(solution)/shard_map/ppermute | solution.py:336
  50.8 12.9 %all-to-all-start = ((bf16[32,8,2944]{2,1,0:T(8,128)(2,1)}), bf16[32,8,2944]{2,1,0:T(8,128)(2,1)S(1)}, u32[]{:S(2)}, u32[]{:S(2)}) async-start(bf16[32,8,2944]{2,1,0:T(8,128)(2,1)} %bitcast.13), calls=%async_computation | async-start | bytes 3014656 | tf_op jit(solution)/shard_map/all_to_all | solution.py:319
  63.8 1.9 collective-permute-start.3
  65.7 4.6 %collective-permute-start.4 = (bf16[144,1280]{1,0:T(8,128)(2,1)S(1)}, bf16[144,1280]{1,0:T(8,128)(2,1)S(1)}, u32[]{:S(2)}, u32[]{:S(2)}) collective-permute-start(bf16[144,1280]{1,0:T(8,128)(2,1)S(1)} %collective-permute-done.refs_2_), channel_id=1, source_target_pairs={{0,390},{1,391},{2,384},{3,385},{4,386},{5,387},{6,388},{7,389},{8... | collective-permute-start | bytes 1105928 | tf_op jit(solution)/shard_map/ppermute | solution.py:336
  70.3 1.9 collective-permute-start.6
  72.3 4.6 %collective-permute-start.9 = (bf16[144,1280]{1,0:T(8,128)(2,1)S(1)}, bf16[144,1280]{1,0:T(8,128)(2,1)S(1)}, u32[]{:S(2)}, u32[]{:S(2)}) collective-permute-start(bf16[144,1280]{1,0:T(8,128)(2,1)S(1)} %collective-permute-done.5.refs_7_), channel_id=1, source_target_pairs={{0,390},{1,391},{2,384},{3,385},{4,386},{5,387},{6,388},{7,389},{8... | collective-permute-start | bytes 1105928 | tf_op jit(solution)/shard_map/ppermute | solution.py:336
  76.9 1.9 collective-permute-start.7
  78.8 4.6 %collective-permute-start.8 = (bf16[144,1280]{1,0:T(8,128)(2,1)S(1)}, bf16[144,1280]{1,0:T(8,128)(2,1)S(1)}, u32[]{:S(2)}, u32[]{:S(2)}) collective-permute-start(bf16[144,1280]{1,0:T(8,128)(2,1)S(1)} %collective-permute-done.4.refs_6_), channel_id=1, source_target_pairs={{0,390},{1,391},{2,384},{3,385},{4,386},{5,387},{6,388},{7,389},{8... | collective-permute-start | bytes 1105928 | tf_op jit(solution)/shard_map/ppermute | solution.py:336
  86.7 4.6 %collective-permute-start.13 = (bf16[144,1280]{1,0:T(8,128)(2,1)S(1)}, bf16[144,1280]{1,0:T(8,128)(2,1)S(1)}, u32[]{:S(2)}, u32[]{:S(2)}) collective-permute-start(bf16[144,1280]{1,0:T(8,128)(2,1)S(1)} %collective-permute-done.9.refs_11_), channel_id=1, source_target_pairs={{0,390},{1,391},{2,384},{3,385},{4,386},{5,387},{6,388},{7,389},{8... | collective-permute-start | bytes 1105928 | tf_op jit(solution)/shard_map/ppermute | solution.py:336
  94.6 4.6 %collective-permute-start.12 = (bf16[144,1280]{1,0:T(8,128)(2,1)S(1)}, bf16[144,1280]{1,0:T(8,128)(2,1)}, u32[]{:S(2)}, u32[]{:S(2)}) collective-permute-start(bf16[144,1280]{1,0:T(8,128)(2,1)S(1)} %collective-permute-done.8.refs_10_), channel_id=1, source_target_pairs={{0,390},{1,391},{2,384},{3,385},{4,386},{5,387},{6,388},{7,389},{8... | collective-permute-start | bytes 1105928 | tf_op jit(solution)/shard_map/ppermute | solution.py:336
  102.5 4.6 %collective-permute-start.17 = (bf16[144,1280]{1,0:T(8,128)(2,1)S(1)}, bf16[144,1280]{1,0:T(8,128)(2,1)}, u32[]{:S(2)}, u32[]{:S(2)}) collective-permute-start(bf16[144,1280]{1,0:T(8,128)(2,1)S(1)} %collective-permute-done.13.refs_15_), channel_id=1, source_target_pairs={{0,390},{1,391},{2,384},{3,385},{4,386},{5,387},{6,388},{7,389},{8... | collective-permute-start | bytes 1105928 | tf_op jit(solution)/shard_map/ppermute | solution.py:336
  110.5 4.6 %collective-permute-start.16 = (bf16[144,1280]{1,0:T(8,128)(2,1)}, bf16[144,1280]{1,0:T(8,128)(2,1)}, u32[]{:S(2)}, u32[]{:S(2)}) collective-permute-start(bf16[144,1280]{1,0:T(8,128)(2,1)} %collective-permute-done.12.refs_14_), channel_id=1, source_target_pairs={{0,390},{1,391},{2,384},{3,385},{4,386},{5,387},{6,388},{7,389},{8... | collective-permute-start | bytes 1105928 | tf_op jit(solution)/shard_map/ppermute | solution.py:336
  118.4 4.6 %collective-permute-start.21 = (bf16[144,1280]{1,0:T(8,128)(2,1)}, bf16[144,1280]{1,0:T(8,128)(2,1)}, u32[]{:S(2)}, u32[]{:S(2)}) collective-permute-start(bf16[144,1280]{1,0:T(8,128)(2,1)} %collective-permute-done.17.refs_19_), channel_id=1, source_target_pairs={{0,390},{1,391},{2,384},{3,385},{4,386},{5,387},{6,388},{7,389},{8... | collective-permute-start | bytes 1105928 | tf_op jit(solution)/shard_map/ppermute | solution.py:336
  123.1 9.5 %all-to-all-start.1 = ((bf16[32,8,2816]{2,1,0:T(8,128)(2,1)}), bf16[32,8,2816]{2,1,0:T(8,128)(2,1)S(1)}, u32[]{:S(2)}, u32[]{:S(2)}) async-start(bf16[32,8,2816]{2,1,0:T(8,128)(2,1)} %bitcast.14), calls=%async_computation.1 | async-start | bytes 2883584 | tf_op jit(solution)/shard_map/all_to_all | solution.py:319
  132.6 1.9 collective-permute-start.19
  134.5 4.6 %collective-permute-start.20 = (bf16[144,1280]{1,0:T(8,128)(2,1)}, bf16[144,1280]{1,0:T(8,128)(2,1)S(1)}, u32[]{:S(2)}, u32[]{:S(2)}) collective-permute-start(bf16[144,1280]{1,0:T(8,128)(2,1)} %collective-permute-done.16.refs_18_), channel_id=1, source_target_pairs={{0,390},{1,391},{2,384},{3,385},{4,386},{5,387},{6,388},{7,389},{8... | collective-permute-start | bytes 1105928 | tf_op jit(solution)/shard_map/ppermute | solution.py:336
  139.1 1.9 collective-permute-start.22
  141.0 4.6 %collective-permute-start.25 = (bf16[144,1280]{1,0:T(8,128)(2,1)}, bf16[144,1280]{1,0:T(8,128)(2,1)S(1)}, u32[]{:S(2)}, u32[]{:S(2)}) collective-permute-start(bf16[144,1280]{1,0:T(8,128)(2,1)} %collective-permute-done.21.refs_23_), channel_id=1, source_target_pairs={{0,390},{1,391},{2,384},{3,385},{4,386},{5,387},{6,388},{7,389},{8... | collective-permute-start | bytes 1105928 | tf_op jit(solution)/shard_map/ppermute | solution.py:336
  147.8 4.6 %collective-permute-start.24 = (bf16[144,1280]{1,0:T(8,128)(2,1)S(1)}, bf16[144,1280]{1,0:T(8,128)(2,1)}, u32[]{:S(2)}, u32[]{:S(2)}) collective-permute-start(bf16[144,1280]{1,0:T(8,128)(2,1)S(1)} %collective-permute-done.20.refs_22_), channel_id=1, source_target_pairs={{0,390},{1,391},{2,384},{3,385},{4,386},{5,387},{6,388},{7,389},{8... | collective-permute-start | bytes 1105928 | tf_op jit(solution)/shard_map/ppermute | solution.py:336
  155.7 4.6 %collective-permute-start.29 = (bf16[144,1280]{1,0:T(8,128)(2,1)S(1)}, bf16[144,1280]{1,0:T(8,128)(2,1)}, u32[]{:S(2)}, u32[]{:S(2)}) collective-permute-start(bf16[144,1280]{1,0:T(8,128)(2,1)S(1)} %collective-permute-done.25.refs_27_), channel_id=1, source_target_pairs={{0,390},{1,391},{2,384},{3,385},{4,386},{5,387},{6,388},{7,389},{8... | collective-permute-start | bytes 1105928 | tf_op jit(solution)/shard_map/ppermute | solution.py:336
  163.7 4.6 %collective-permute-start.28 = (bf16[144,1280]{1,0:T(8,128)(2,1)}, bf16[144,1280]{1,0:T(8,128)(2,1)}, u32[]{:S(2)}, u32[]{:S(2)}) collective-permute-start(bf16[144,1280]{1,0:T(8,128)(2,1)} %collective-permute-done.24.refs_26_), channel_id=1, source_target_pairs={{0,390},{1,391},{2,384},{3,385},{4,386},{5,387},{6,388},{7,389},{8... | collective-permute-start | bytes 1105928 | tf_op jit(solution)/shard_map/ppermute | solution.py:336
  171.6 4.8 %collective-permute-start.31 = (bf16[144,1280]{1,0:T(8,128)(2,1)}, bf16[144,1280]{1,0:T(8,128)(2,1)}, u32[]{:S(2)}, u32[]{:S(2)}) collective-permute-start(bf16[144,1280]{1,0:T(8,128)(2,1)} %collective-permute-done.29.refs_31_), channel_id=1, source_target_pairs={{0,390},{1,391},{2,384},{3,385},{4,386},{5,387},{6,388},{7,389},{8... | collective-permute-start | bytes 1105928 | tf_op jit(solution)/shard_map/ppermute | solution.py:338
  178.4 7.0 %collective-permute-done.30.refs_32_ = bf16[144,1280]{1,0:T(8,128)(2,1)} collective-permute-done((bf16[144,1280]{1,0:T(8,128)(2,1)}, bf16[144,1280]{1,0:T(8,128)(2,1)}, u32[]{:S(2)}, u32[]{:S(2)}) %collective-permute-start.30) | collective-permute-done | bytes 368672 | tf_op jit(solution)/shard_map/ppermute | solution.py:338
  186.3 14.0 %shard_map.87 = bf16[256,2944]{1,0:T(8,128)(2,1)} custom-call(bf16[256,2944]{1,0:T(8,128)(2,1)} %bitcast.10, bf16[256,2816]{1,0:T(8,128)(2,1)} %bitcast.12, bf16[144,1280]{1,0:T(8,128)(2,1)} %copy-done.4, bf16[144,1280]{1,0:T(8,128)(2,1)} %copy-done.5, bf16[144,1280]{1,0:T(8,128)(2,1)} %copy-done.6, bf16[144,1280]{1,0:T(8,128)(2,1)} %copy-done.8, ...), custom_call_target="tpu_custom_call" | custom-call | tf_op jit(solution)/shard_map/pallas_call | solution.py:212
  200.3 8.5 %all-to-all-start.2 = ((bf16[32,8,2944]{2,1,0:T(8,128)(2,1)}), bf16[32,8,2944]{2,1,0:T(8,128)(2,1)S(1)}, u32[]{:S(2)}, u32[]{:S(2)}) async-start(bf16[32,8,2944]{2,1,0:T(8,128)(2,1)} %bitcast.11), calls=%async_computation.2 | async-start | bytes 3014656 | tf_op jit(solution)/shard_map/all_to_all | solution.py:319
  209.0 21.3 %all-to-all-done.2 = bf16[32,8,2944]{2,1,0:T(8,128)(2,1)S(1)} async-done(((bf16[32,8,2944]{2,1,0:T(8,128)(2,1)}), bf16[32,8,2944]{2,1,0:T(8,128)(2,1)S(1)}, u32[]{:S(2)}, u32[]{:S(2)}) %all-to-all-start.2) | async-done | bytes 1507360 | tf_op jit(solution)/shard_map/all_to_all | solution.py:319
  230.3 2.0 shard_map.88
  (90 shorter events, 34.4 us)
Async XLA Ops:
  1.9 25.5 %collective-permute-start = (bf16[144,1280]{1,0:T(8,128)(2,1)S(1)}, bf16[144,1280]{1,0:T(8,128)(2,1)S(1)}, u32[]{:S(2)}, u32[]{:S(2)}) collective-permute-start(bf16[144,1280]{1,0:T(8,128)(2,1)S(1)} %get-tuple-element.17), channel_id=1, source_target_pairs={{0,260},{1,261},{2,294},{3,295},{4,320},{5,321},{6,354},{7,355},{8... | collective-permute-start | bytes 1105928 | tf_op jit(solution)/shard_map/ppermute | solution.py:329
  17.3 20.6 %collective-permute-start.1 = (bf16[144,1280]{1,0:T(8,128)(2,1)S(1)}, bf16[144,1280]{1,0:T(8,128)(2,1)S(1)}, u32[]{:S(2)}, u32[]{:S(2)}) collective-permute-start(bf16[144,1280]{1,0:T(8,128)(2,1)S(1)} %get-tuple-element.16), channel_id=1, source_target_pairs={{0,260},{1,261},{2,294},{3,295},{4,320},{5,321},{6,354},{7,355},{8... | collective-permute-start | bytes 1105928 | tf_op jit(solution)/shard_map/ppermute | solution.py:329
  27.5 42.8 %collective-permute-start.2 = (bf16[144,1280]{1,0:T(8,128)(2,1)S(1)}, bf16[144,1280]{1,0:T(8,128)(2,1)S(1)}, u32[]{:S(2)}, u32[]{:S(2)}) collective-permute-start(bf16[144,1280]{1,0:T(8,128)(2,1)S(1)} %collective-permute-done.refs_2_), channel_id=1, source_target_pairs={{0,128},{1,129},{2,130},{3,131},{4,132},{5,133},{6,134},{7,135},{8... | collective-permute-start | bytes 1105928 | tf_op jit(solution)/shard_map/ppermute | solution.py:335
  37.9 34.4 %collective-permute-start.5 = (bf16[144,1280]{1,0:T(8,128)(2,1)S(1)}, bf16[144,1280]{1,0:T(8,128)(2,1)S(1)}, u32[]{:S(2)}, u32[]{:S(2)}) collective-permute-start(bf16[144,1280]{1,0:T(8,128)(2,1)S(1)} %collective-permute-done.1.refs_3_), channel_id=1, source_target_pairs={{0,390},{1,391},{2,384},{3,385},{4,386},{5,387},{6,388},{7,389},{8... | collective-permute-start | bytes 1105928 | tf_op jit(solution)/shard_map/ppermute | solution.py:336
  50.8 72.2 %all-to-all-start = ((bf16[32,8,2944]{2,1,0:T(8,128)(2,1)}), bf16[32,8,2944]{2,1,0:T(8,128)(2,1)S(1)}, u32[]{:S(2)}, u32[]{:S(2)}) async-start(bf16[32,8,2944]{2,1,0:T(8,128)(2,1)} %bitcast.13), calls=%async_computation | async-start | bytes 3014656 | tf_op jit(solution)/shard_map/all_to_all | solution.py:319
  70.3 14.4 %collective-permute-start.6 = (bf16[144,1280]{1,0:T(8,128)(2,1)S(1)}, bf16[144,1280]{1,0:T(8,128)(2,1)S(1)}, u32[]{:S(2)}, u32[]{:S(2)}) collective-permute-start(bf16[144,1280]{1,0:T(8,128)(2,1)S(1)} %collective-permute-done.2.refs_4_), channel_id=1, source_target_pairs={{0,128},{1,129},{2,130},{3,131},{4,132},{5,133},{6,134},{7,135},{8... | collective-permute-start | bytes 1105928 | tf_op jit(solution)/shard_map/ppermute | solution.py:335
  72.3 14.4 %collective-permute-start.9 = (bf16[144,1280]{1,0:T(8,128)(2,1)S(1)}, bf16[144,1280]{1,0:T(8,128)(2,1)S(1)}, u32[]{:S(2)}, u32[]{:S(2)}) collective-permute-start(bf16[144,1280]{1,0:T(8,128)(2,1)S(1)} %collective-permute-done.5.refs_7_), channel_id=1, source_target_pairs={{0,390},{1,391},{2,384},{3,385},{4,386},{5,387},{6,388},{7,389},{8... | collective-permute-start | bytes 1105928 | tf_op jit(solution)/shard_map/ppermute | solution.py:336
  76.9 15.8 %collective-permute-start.7 = (bf16[144,1280]{1,0:T(8,128)(2,1)S(1)}, bf16[144,1280]{1,0:T(8,128)(2,1)S(1)}, u32[]{:S(2)}, u32[]{:S(2)}) collective-permute-start(bf16[144,1280]{1,0:T(8,128)(2,1)S(1)} %collective-permute-done.3.refs_5_), channel_id=1, source_target_pairs={{0,128},{1,129},{2,130},{3,131},{4,132},{5,133},{6,134},{7,135},{8... | collective-permute-start | bytes 1105928 | tf_op jit(solution)/shard_map/ppermute | solution.py:335
  78.8 15.7 %collective-permute-start.8 = (bf16[144,1280]{1,0:T(8,128)(2,1)S(1)}, bf16[144,1280]{1,0:T(8,128)(2,1)S(1)}, u32[]{:S(2)}, u32[]{:S(2)}) collective-permute-start(bf16[144,1280]{1,0:T(8,128)(2,1)S(1)} %collective-permute-done.4.refs_6_), channel_id=1, source_target_pairs={{0,390},{1,391},{2,384},{3,385},{4,386},{5,387},{6,388},{7,389},{8... | collective-permute-start | bytes 1105928 | tf_op jit(solution)/shard_map/ppermute | solution.py:336
  84.7 15.8 %collective-permute-start.10 = (bf16[144,1280]{1,0:T(8,128)(2,1)S(1)}, bf16[144,1280]{1,0:T(8,128)(2,1)S(1)}, u32[]{:S(2)}, u32[]{:S(2)}) collective-permute-start(bf16[144,1280]{1,0:T(8,128)(2,1)S(1)} %collective-permute-done.6.refs_8_), channel_id=1, source_target_pairs={{0,128},{1,129},{2,130},{3,131},{4,132},{5,133},{6,134},{7,135},{8... | collective-permute-start | bytes 1105928 | tf_op jit(solution)/shard_map/ppermute | solution.py:335
  86.7 15.8 %collective-permute-start.13 = (bf16[144,1280]{1,0:T(8,128)(2,1)S(1)}, bf16[144,1280]{1,0:T(8,128)(2,1)S(1)}, u32[]{:S(2)}, u32[]{:S(2)}) collective-permute-start(bf16[144,1280]{1,0:T(8,128)(2,1)S(1)} %collective-permute-done.9.refs_11_), channel_id=1, source_target_pairs={{0,390},{1,391},{2,384},{3,385},{4,386},{5,387},{6,388},{7,389},{8... | collective-permute-start | bytes 1105928 | tf_op jit(solution)/shard_map/ppermute | solution.py:336
  92.6 15.9 %collective-permute-start.11 = (bf16[144,1280]{1,0:T(8,128)(2,1)S(1)}, bf16[144,1280]{1,0:T(8,128)(2,1)}, u32[]{:S(2)}, u32[]{:S(2)}) collective-permute-start(bf16[144,1280]{1,0:T(8,128)(2,1)S(1)} %collective-permute-done.7.refs_9_), channel_id=1, source_target_pairs={{0,128},{1,129},{2,130},{3,131},{4,132},{5,133},{6,134},{7,135},{8... | collective-permute-start | bytes 1105928 | tf_op jit(solution)/shard_map/ppermute | solution.py:335
  94.6 15.9 %collective-permute-start.12 = (bf16[144,1280]{1,0:T(8,128)(2,1)S(1)}, bf16[144,1280]{1,0:T(8,128)(2,1)}, u32[]{:S(2)}, u32[]{:S(2)}) collective-permute-start(bf16[144,1280]{1,0:T(8,128)(2,1)S(1)} %collective-permute-done.8.refs_10_), channel_id=1, source_target_pairs={{0,390},{1,391},{2,384},{3,385},{4,386},{5,387},{6,388},{7,389},{8... | collective-permute-start | bytes 1105928 | tf_op jit(solution)/shard_map/ppermute | solution.py:336
  100.5 15.9 %collective-permute-start.14 = (bf16[144,1280]{1,0:T(8,128)(2,1)S(1)}, bf16[144,1280]{1,0:T(8,128)(2,1)}, u32[]{:S(2)}, u32[]{:S(2)}) collective-permute-start(bf16[144,1280]{1,0:T(8,128)(2,1)S(1)} %collective-permute-done.10.refs_12_), channel_id=1, source_target_pairs={{0,128},{1,129},{2,130},{3,131},{4,132},{5,133},{6,134},{7,135},{8... | collective-permute-start | bytes 1105928 | tf_op jit(solution)/shard_map/ppermute | solution.py:335
  102.5 15.9 %collective-permute-start.17 = (bf16[144,1280]{1,0:T(8,128)(2,1)S(1)}, bf16[144,1280]{1,0:T(8,128)(2,1)}, u32[]{:S(2)}, u32[]{:S(2)}) collective-permute-start(bf16[144,1280]{1,0:T(8,128)(2,1)S(1)} %collective-permute-done.13.refs_15_), channel_id=1, source_target_pairs={{0,390},{1,391},{2,384},{3,385},{4,386},{5,387},{6,388},{7,389},{8... | collective-permute-start | bytes 1105928 | tf_op jit(solution)/shard_map/ppermute | solution.py:336
  108.6 24.0 %collective-permute-start.15 = (bf16[144,1280]{1,0:T(8,128)(2,1)}, bf16[144,1280]{1,0:T(8,128)(2,1)}, u32[]{:S(2)}, u32[]{:S(2)}) collective-permute-start(bf16[144,1280]{1,0:T(8,128)(2,1)} %collective-permute-done.11.refs_13_), channel_id=1, source_target_pairs={{0,128},{1,129},{2,130},{3,131},{4,132},{5,133},{6,134},{7,135},{8... | collective-permute-start | bytes 1105928 | tf_op jit(solution)/shard_map/ppermute | solution.py:335
  110.5 24.0 %collective-permute-start.16 = (bf16[144,1280]{1,0:T(8,128)(2,1)}, bf16[144,1280]{1,0:T(8,128)(2,1)}, u32[]{:S(2)}, u32[]{:S(2)}) collective-permute-start(bf16[144,1280]{1,0:T(8,128)(2,1)} %collective-permute-done.12.refs_14_), channel_id=1, source_target_pairs={{0,390},{1,391},{2,384},{3,385},{4,386},{5,387},{6,388},{7,389},{8... | collective-permute-start | bytes 1105928 | tf_op jit(solution)/shard_map/ppermute | solution.py:336
  116.5 22.6 %collective-permute-start.18 = (bf16[144,1280]{1,0:T(8,128)(2,1)}, bf16[144,1280]{1,0:T(8,128)(2,1)}, u32[]{:S(2)}, u32[]{:S(2)}) collective-permute-start(bf16[144,1280]{1,0:T(8,128)(2,1)} %collective-permute-done.14.refs_16_), channel_id=1, source_target_pairs={{0,128},{1,129},{2,130},{3,131},{4,132},{5,133},{6,134},{7,135},{8... | collective-permute-start | bytes 1105928 | tf_op jit(solution)/shard_map/ppermute | solution.py:335
  118.4 22.6 %collective-permute-start.21 = (bf16[144,1280]{1,0:T(8,128)(2,1)}, bf16[144,1280]{1,0:T(8,128)(2,1)}, u32[]{:S(2)}, u32[]{:S(2)}) collective-permute-start(bf16[144,1280]{1,0:T(8,128)(2,1)} %collective-permute-done.17.refs_19_), channel_id=1, source_target_pairs={{0,390},{1,391},{2,384},{3,385},{4,386},{5,387},{6,388},{7,389},{8... | collective-permute-start | bytes 1105928 | tf_op jit(solution)/shard_map/ppermute | solution.py:336
  123.1 53.3 %all-to-all-start.1 = ((bf16[32,8,2816]{2,1,0:T(8,128)(2,1)}), bf16[32,8,2816]{2,1,0:T(8,128)(2,1)S(1)}, u32[]{:S(2)}, u32[]{:S(2)}) async-start(bf16[32,8,2816]{2,1,0:T(8,128)(2,1)} %bitcast.14), calls=%async_computation.1 | async-start | bytes 2883584 | tf_op jit(solution)/shard_map/all_to_all | solution.py:319
  132.6 13.3 %collective-permute-start.19 = (bf16[144,1280]{1,0:T(8,128)(2,1)}, bf16[144,1280]{1,0:T(8,128)(2,1)S(1)}, u32[]{:S(2)}, u32[]{:S(2)}) collective-permute-start(bf16[144,1280]{1,0:T(8,128)(2,1)} %collective-permute-done.15.refs_17_), channel_id=1, source_target_pairs={{0,128},{1,129},{2,130},{3,131},{4,132},{5,133},{6,134},{7,135},{8... | collective-permute-start | bytes 1105928 | tf_op jit(solution)/shard_map/ppermute | solution.py:335
  139.1 14.6 %collective-permute-start.22 = (bf16[144,1280]{1,0:T(8,128)(2,1)}, bf16[144,1280]{1,0:T(8,128)(2,1)S(1)}, u32[]{:S(2)}, u32[]{:S(2)}) collective-permute-start(bf16[144,1280]{1,0:T(8,128)(2,1)} %collective-permute-done.18.refs_20_), channel_id=1, source_target_pairs={{0,128},{1,129},{2,130},{3,131},{4,132},{5,133},{6,134},{7,135},{8... | collective-permute-start | bytes 1105928 | tf_op jit(solution)/shard_map/ppermute | solution.py:335
  141.0 14.6 %collective-permute-start.25 = (bf16[144,1280]{1,0:T(8,128)(2,1)}, bf16[144,1280]{1,0:T(8,128)(2,1)S(1)}, u32[]{:S(2)}, u32[]{:S(2)}) collective-permute-start(bf16[144,1280]{1,0:T(8,128)(2,1)} %collective-permute-done.21.refs_23_), channel_id=1, source_target_pairs={{0,390},{1,391},{2,384},{3,385},{4,386},{5,387},{6,388},{7,389},{8... | collective-permute-start | bytes 1105928 | tf_op jit(solution)/shard_map/ppermute | solution.py:336
  145.8 15.9 %collective-permute-start.23 = (bf16[144,1280]{1,0:T(8,128)(2,1)S(1)}, bf16[144,1280]{1,0:T(8,128)(2,1)}, u32[]{:S(2)}, u32[]{:S(2)}) collective-permute-start(bf16[144,1280]{1,0:T(8,128)(2,1)S(1)} %collective-permute-done.19.refs_21_), channel_id=1, source_target_pairs={{0,128},{1,129},{2,130},{3,131},{4,132},{5,133},{6,134},{7,135},{8... | collective-permute-start | bytes 1105928 | tf_op jit(solution)/shard_map/ppermute | solution.py:335
  147.8 15.9 %collective-permute-start.24 = (bf16[144,1280]{1,0:T(8,128)(2,1)S(1)}, bf16[144,1280]{1,0:T(8,128)(2,1)}, u32[]{:S(2)}, u32[]{:S(2)}) collective-permute-start(bf16[144,1280]{1,0:T(8,128)(2,1)S(1)} %collective-permute-done.20.refs_22_), channel_id=1, source_target_pairs={{0,390},{1,391},{2,384},{3,385},{4,386},{5,387},{6,388},{7,389},{8... | collective-permute-start | bytes 1105928 | tf_op jit(solution)/shard_map/ppermute | solution.py:336
  153.7 15.9 %collective-permute-start.26 = (bf16[144,1280]{1,0:T(8,128)(2,1)S(1)}, bf16[144,1280]{1,0:T(8,128)(2,1)}, u32[]{:S(2)}, u32[]{:S(2)}) collective-permute-start(bf16[144,1280]{1,0:T(8,128)(2,1)S(1)} %collective-permute-done.22.refs_24_), channel_id=1, source_target_pairs={{0,128},{1,129},{2,130},{3,131},{4,132},{5,133},{6,134},{7,135},{8... | collective-permute-start | bytes 1105928 | tf_op jit(solution)/shard_map/ppermute | solution.py:335
  155.7 15.9 %collective-permute-start.29 = (bf16[144,1280]{1,0:T(8,128)(2,1)S(1)}, bf16[144,1280]{1,0:T(8,128)(2,1)}, u32[]{:S(2)}, u32[]{:S(2)}) collective-permute-start(bf16[144,1280]{1,0:T(8,128)(2,1)S(1)} %collective-permute-done.25.refs_27_), channel_id=1, source_target_pairs={{0,390},{1,391},{2,384},{3,385},{4,386},{5,387},{6,388},{7,389},{8... | collective-permute-start | bytes 1105928 | tf_op jit(solution)/shard_map/ppermute | solution.py:336
  161.7 15.8 %collective-permute-start.27 = (bf16[144,1280]{1,0:T(8,128)(2,1)}, bf16[144,1280]{1,0:T(8,128)(2,1)}, u32[]{:S(2)}, u32[]{:S(2)}) collective-permute-start(bf16[144,1280]{1,0:T(8,128)(2,1)} %collective-permute-done.23.refs_25_), channel_id=1, source_target_pairs={{0,128},{1,129},{2,130},{3,131},{4,132},{5,133},{6,134},{7,135},{8... | collective-permute-start | bytes 1105928 | tf_op jit(solution)/shard_map/ppermute | solution.py:335
  163.7 14.7 %collective-permute-start.28 = (bf16[144,1280]{1,0:T(8,128)(2,1)}, bf16[144,1280]{1,0:T(8,128)(2,1)}, u32[]{:S(2)}, u32[]{:S(2)}) collective-permute-start(bf16[144,1280]{1,0:T(8,128)(2,1)} %collective-permute-done.24.refs_26_), channel_id=1, source_target_pairs={{0,390},{1,391},{2,384},{3,385},{4,386},{5,387},{6,388},{7,389},{8... | collective-permute-start | bytes 1105928 | tf_op jit(solution)/shard_map/ppermute | solution.py:336
  169.6 15.8 %collective-permute-start.30 = (bf16[144,1280]{1,0:T(8,128)(2,1)}, bf16[144,1280]{1,0:T(8,128)(2,1)}, u32[]{:S(2)}, u32[]{:S(2)}) collective-permute-start(bf16[144,1280]{1,0:T(8,128)(2,1)} %collective-permute-done.26.refs_28_), channel_id=1, source_target_pairs={{0,128},{1,129},{2,130},{3,131},{4,132},{5,133},{6,134},{7,135},{8... | collective-permute-start | bytes 1105928 | tf_op jit(solution)/shard_map/ppermute | solution.py:338
  171.6 14.7 %collective-permute-start.31 = (bf16[144,1280]{1,0:T(8,128)(2,1)}, bf16[144,1280]{1,0:T(8,128)(2,1)}, u32[]{:S(2)}, u32[]{:S(2)}) collective-permute-start(bf16[144,1280]{1,0:T(8,128)(2,1)} %collective-permute-done.29.refs_31_), channel_id=1, source_target_pairs={{0,390},{1,391},{2,384},{3,385},{4,386},{5,387},{6,388},{7,389},{8... | collective-permute-start | bytes 1105928 | tf_op jit(solution)/shard_map/ppermute | solution.py:338
  200.3 29.9 %all-to-all-start.2 = ((bf16[32,8,2944]{2,1,0:T(8,128)(2,1)}), bf16[32,8,2944]{2,1,0:T(8,128)(2,1)S(1)}, u32[]{:S(2)}, u32[]{:S(2)}) async-start(bf16[32,8,2944]{2,1,0:T(8,128)(2,1)} %bitcast.11), calls=%async_computation.2 | async-start | bytes 3014656 | tf_op jit(solution)/shard_map/all_to_all | solution.py:319
  (25 other events, 751.3 us)

commit v4 on v3

--- a/solution.py
+++ b/solution.py
@@ -248,7 +248,7 @@
         low = jnp.where(mine < LANES, mine + LANES, 17)
         high = jnp.where(mine < LANES, mine, 16)
         terms.append(jnp.sum(jnp.where((lane == high) | (lane == low), got, 0.0), axis=1, keepdims=True))
-    term_ref[...] = jnp.where(iota((tok_rows, 2), 1) == 0, terms[0], terms[1])
+    term_ref[...] = jnp.where(lane == 0, terms[0], terms[1]).T[:2]
 
 
 def bring_home(home, base, slot, gates, width):
@@ -257,7 +257,7 @@
         home_kernel,
         out_shape=(
             jax.ShapeDtypeStruct((tok_rows, width), BF16),
-            jax.ShapeDtypeStruct((tok_rows, 2), F32),
+            jax.ShapeDtypeStruct((2, tok_rows), F32),
         ),
         in_specs=[pl.BlockSpec(memory_space=pltpu.VMEM)] * 4,
         out_specs=[pl.BlockSpec(memory_space=pltpu.VMEM)] * 2,
@@ -341,7 +341,8 @@
     total = None
     for begin, end in PARTS:
         total = expert_part(wires, slices[begin:end], total, end == len(slices))
-    return bring_home(exchange(total), base, slot, gate_values, width)
+    token_grad, terms = bring_home(exchange(total), base, slot, gate_values, width)
+    return token_grad, terms.T
 
 
 def solution(mesh):

time: 234 us -> 234 us (level)
  no operation moved by 1% of the time
where the time goes in v4:
time: 234 us; the launch traced here: 232 us
  starting transfers between devices  157 us (67%)
  waiting for transfers between devices  51.2 us (22%)
  Pallas kernels  20.7 us (9%)
    ppermute x14, starting transfers between devices, local(): left = [lax.ppermute(part, AXES, down) for part in left]  72.4 us
    all_to_all x3, starting transfers between devices, exchange(): got = lax.all_to_all(sent, PLANE, split_axis=0, concat_axis=0, tiled=True)  30.9 us
    ppermute x14, starting transfers between devices, local(): right = [lax.ppermute(part, AXES, up) for part in right]  26.8 us
    all_to_all x3, waiting for transfers between devices, exchange(): got = lax.all_to_all(sent, PLANE, split_axis=0, concat_axis=0, tiled=True)  21.3 us
    ppermute x2, starting transfers between devices, local(): lax.ppermute(part, AXES, spread)  20 us
    pallas_call x1, Pallas kernels, expert_part(): pl.pallas_call(functools.partial(expert_kernel, count, first, last), out_...  14 us
    ppermute x14, waiting for transfers between devices, local(): right = [lax.ppermute(part, AXES, up) for part in right]  12.6 us
    ppermute x2, waiting for transfers between devices, local(): lax.ppermute(part, AXES, spread)  8.49 us
  transfers between devices with their start and end apart: 35, of which 15 were waited for; matrix products, arithmetic and copies ran while one was open for 0% of the time, Pallas kernels for 2%

profile of v4, /device:TPU:1, one launch (start us, length us, event | category | flops | bytes accessed | tf_op | source)
XLA Modules:
  0.0 232.2 jit_solution(10662695046615075049)
XLA Ops:
  1.9 15.4 %collective-permute-start = (bf16[144,1280]{1,0:T(8,128)(2,1)S(1)}, bf16[144,1280]{1,0:T(8,128)(2,1)S(1)}, u32[]{:S(2)}, u32[]{:S(2)}) collective-permute-start(bf16[144,1280]{1,0:T(8,128)(2,1)S(1)} %get-tuple-element.19), channel_id=1, source_target_pairs={{0,260},{1,261},{2,294},{3,295},{4,320},{5,321},{6,354},{7,355},{8... | collective-permute-start | bytes 1105928 | tf_op jit(solution)/shard_map/ppermute | solution.py:329
  17.3 4.7 %collective-permute-start.1 = (bf16[144,1280]{1,0:T(8,128)(2,1)S(1)}, bf16[144,1280]{1,0:T(8,128)(2,1)S(1)}, u32[]{:S(2)}, u32[]{:S(2)}) collective-permute-start(bf16[144,1280]{1,0:T(8,128)(2,1)S(1)} %get-tuple-element.18), channel_id=1, source_target_pairs={{0,260},{1,261},{2,294},{3,295},{4,320},{5,321},{6,354},{7,355},{8... | collective-permute-start | bytes 1105928 | tf_op jit(solution)/shard_map/ppermute | solution.py:329
  22.7 4.7 %shard_map.86 = (bf16[256,2944]{1,0:T(8,128)(2,1)}, bf16[256,2816]{1,0:T(8,128)(2,1)}, s32[128,2]{1,0:T(8,128)}, s32[128,2]{1,0:T(8,128)}) custom-call(bf16[128,2560]{1,0:T(8,128)(2,1)} %tokens_ref.1, bf16[128,2560]{1,0:T(8,128)(2,1)} %cotangent_ref.1, s32[128,2]{1,0:T(8,128)} %copy.9.ids_ref), custom_call_target="tpu_custom_call" | custom-call | tf_op jit(solution)/shard_map/pallas_call | solution.py:303
  27.5 1.9 collective-permute-start.2
  29.4 8.5 %collective-permute-done.1.refs_3_ = bf16[144,1280]{1,0:T(8,128)(2,1)S(1)} collective-permute-done((bf16[144,1280]{1,0:T(8,128)(2,1)S(1)}, bf16[144,1280]{1,0:T(8,128)(2,1)S(1)}, u32[]{:S(2)}, u32[]{:S(2)}) %collective-permute-start.1) | collective-permute-done | bytes 368672 | tf_op jit(solution)/shard_map/ppermute | solution.py:329
  37.9 12.9 %collective-permute-start.5 = (bf16[144,1280]{1,0:T(8,128)(2,1)S(1)}, bf16[144,1280]{1,0:T(8,128)(2,1)S(1)}, u32[]{:S(2)}, u32[]{:S(2)}) collective-permute-start(bf16[144,1280]{1,0:T(8,128)(2,1)S(1)} %collective-permute-done.1.refs_3_), channel_id=1, source_target_pairs={{0,390},{1,391},{2,384},{3,385},{4,386},{5,387},{6,388},{7,389},{8... | collective-permute-start | bytes 1105928 | tf_op jit(solution)/shard_map/ppermute | solution.py:336
  50.8 12.9 %all-to-all-start = ((bf16[32,8,2944]{2,1,0:T(8,128)(2,1)}), bf16[32,8,2944]{2,1,0:T(8,128)(2,1)S(1)}, u32[]{:S(2)}, u32[]{:S(2)}) async-start(bf16[32,8,2944]{2,1,0:T(8,128)(2,1)} %bitcast.14), calls=%async_computation | async-start | bytes 3014656 | tf_op jit(solution)/shard_map/all_to_all | solution.py:319
  63.8 1.9 collective-permute-start.3
  65.7 4.6 %collective-permute-start.4 = (bf16[144,1280]{1,0:T(8,128)(2,1)S(1)}, bf16[144,1280]{1,0:T(8,128)(2,1)S(1)}, u32[]{:S(2)}, u32[]{:S(2)}) collective-permute-start(bf16[144,1280]{1,0:T(8,128)(2,1)S(1)} %collective-permute-done.refs_2_), channel_id=1, source_target_pairs={{0,390},{1,391},{2,384},{3,385},{4,386},{5,387},{6,388},{7,389},{8... | collective-permute-start | bytes 1105928 | tf_op jit(solution)/shard_map/ppermute | solution.py:336
  70.3 1.9 collective-permute-start.6
  72.3 4.6 %collective-permute-start.9 = (bf16[144,1280]{1,0:T(8,128)(2,1)S(1)}, bf16[144,1280]{1,0:T(8,128)(2,1)S(1)}, u32[]{:S(2)}, u32[]{:S(2)}) collective-permute-start(bf16[144,1280]{1,0:T(8,128)(2,1)S(1)} %collective-permute-done.5.refs_7_), channel_id=1, source_target_pairs={{0,390},{1,391},{2,384},{3,385},{4,386},{5,387},{6,388},{7,389},{8... | collective-permute-start | bytes 1105928 | tf_op jit(solution)/shard_map/ppermute | solution.py:336
  76.9 1.9 collective-permute-start.7
  78.8 4.6 %collective-permute-start.8 = (bf16[144,1280]{1,0:T(8,128)(2,1)S(1)}, bf16[144,1280]{1,0:T(8,128)(2,1)S(1)}, u32[]{:S(2)}, u32[]{:S(2)}) collective-permute-start(bf16[144,1280]{1,0:T(8,128)(2,1)S(1)} %collective-permute-done.4.refs_6_), channel_id=1, source_target_pairs={{0,390},{1,391},{2,384},{3,385},{4,386},{5,387},{6,388},{7,389},{8... | collective-permute-start | bytes 1105928 | tf_op jit(solution)/shard_map/ppermute | solution.py:336
  86.7 4.6 %collective-permute-start.13 = (bf16[144,1280]{1,0:T(8,128)(2,1)S(1)}, bf16[144,1280]{1,0:T(8,128)(2,1)S(1)}, u32[]{:S(2)}, u32[]{:S(2)}) collective-permute-start(bf16[144,1280]{1,0:T(8,128)(2,1)S(1)} %collective-permute-done.9.refs_11_), channel_id=1, source_target_pairs={{0,390},{1,391},{2,384},{3,385},{4,386},{5,387},{6,388},{7,389},{8... | collective-permute-start | bytes 1105928 | tf_op jit(solution)/shard_map/ppermute | solution.py:336
  94.6 4.6 %collective-permute-start.12 = (bf16[144,1280]{1,0:T(8,128)(2,1)S(1)}, bf16[144,1280]{1,0:T(8,128)(2,1)}, u32[]{:S(2)}, u32[]{:S(2)}) collective-permute-start(bf16[144,1280]{1,0:T(8,128)(2,1)S(1)} %collective-permute-done.8.refs_10_), channel_id=1, source_target_pairs={{0,390},{1,391},{2,384},{3,385},{4,386},{5,387},{6,388},{7,389},{8... | collective-permute-start | bytes 1105928 | tf_op jit(solution)/shard_map/ppermute | solution.py:336
  102.5 4.6 %collective-permute-start.17 = (bf16[144,1280]{1,0:T(8,128)(2,1)S(1)}, bf16[144,1280]{1,0:T(8,128)(2,1)}, u32[]{:S(2)}, u32[]{:S(2)}) collective-permute-start(bf16[144,1280]{1,0:T(8,128)(2,1)S(1)} %collective-permute-done.13.refs_15_), channel_id=1, source_target_pairs={{0,390},{1,391},{2,384},{3,385},{4,386},{5,387},{6,388},{7,389},{8... | collective-permute-start | bytes 1105928 | tf_op jit(solution)/shard_map/ppermute | solution.py:336
  110.5 4.6 %collective-permute-start.16 = (bf16[144,1280]{1,0:T(8,128)(2,1)}, bf16[144,1280]{1,0:T(8,128)(2,1)}, u32[]{:S(2)}, u32[]{:S(2)}) collective-permute-start(bf16[144,1280]{1,0:T(8,128)(2,1)} %collective-permute-done.12.refs_14_), channel_id=1, source_target_pairs={{0,390},{1,391},{2,384},{3,385},{4,386},{5,387},{6,388},{7,389},{8... | collective-permute-start | bytes 1105928 | tf_op jit(solution)/shard_map/ppermute | solution.py:336
  118.4 4.6 %collective-permute-start.21 = (bf16[144,1280]{1,0:T(8,128)(2,1)}, bf16[144,1280]{1,0:T(8,128)(2,1)}, u32[]{:S(2)}, u32[]{:S(2)}) collective-permute-start(bf16[144,1280]{1,0:T(8,128)(2,1)} %collective-permute-done.17.refs_19_), channel_id=1, source_target_pairs={{0,390},{1,391},{2,384},{3,385},{4,386},{5,387},{6,388},{7,389},{8... | collective-permute-start | bytes 1105928 | tf_op jit(solution)/shard_map/ppermute | solution.py:336
  123.1 9.5 %all-to-all-start.1 = ((bf16[32,8,2816]{2,1,0:T(8,128)(2,1)}), bf16[32,8,2816]{2,1,0:T(8,128)(2,1)S(1)}, u32[]{:S(2)}, u32[]{:S(2)}) async-start(bf16[32,8,2816]{2,1,0:T(8,128)(2,1)} %bitcast.15), calls=%async_computation.1 | async-start | bytes 2883584 | tf_op jit(solution)/shard_map/all_to_all | solution.py:319
  132.5 1.9 collective-permute-start.19
  134.5 4.6 %collective-permute-start.20 = (bf16[144,1280]{1,0:T(8,128)(2,1)}, bf16[144,1280]{1,0:T(8,128)(2,1)S(1)}, u32[]{:S(2)}, u32[]{:S(2)}) collective-permute-start(bf16[144,1280]{1,0:T(8,128)(2,1)} %collective-permute-done.16.refs_18_), channel_id=1, source_target_pairs={{0,390},{1,391},{2,384},{3,385},{4,386},{5,387},{6,388},{7,389},{8... | collective-permute-start | bytes 1105928 | tf_op jit(solution)/shard_map/ppermute | solution.py:336
  139.1 1.9 collective-permute-start.22
  141.0 4.6 %collective-permute-start.25 = (bf16[144,1280]{1,0:T(8,128)(2,1)}, bf16[144,1280]{1,0:T(8,128)(2,1)S(1)}, u32[]{:S(2)}, u32[]{:S(2)}) collective-permute-start(bf16[144,1280]{1,0:T(8,128)(2,1)} %collective-permute-done.21.refs_23_), channel_id=1, source_target_pairs={{0,390},{1,391},{2,384},{3,385},{4,386},{5,387},{6,388},{7,389},{8... | collective-permute-start | bytes 1105928 | tf_op jit(solution)/shard_map/ppermute | solution.py:336
  147.8 4.6 %collective-permute-start.24 = (bf16[144,1280]{1,0:T(8,128)(2,1)S(1)}, bf16[144,1280]{1,0:T(8,128)(2,1)}, u32[]{:S(2)}, u32[]{:S(2)}) collective-permute-start(bf16[144,1280]{1,0:T(8,128)(2,1)S(1)} %collective-permute-done.20.refs_22_), channel_id=1, source_target_pairs={{0,390},{1,391},{2,384},{3,385},{4,386},{5,387},{6,388},{7,389},{8... | collective-permute-start | bytes 1105928 | tf_op jit(solution)/shard_map/ppermute | solution.py:336
  155.7 4.6 %collective-permute-start.29 = (bf16[144,1280]{1,0:T(8,128)(2,1)S(1)}, bf16[144,1280]{1,0:T(8,128)(2,1)}, u32[]{:S(2)}, u32[]{:S(2)}) collective-permute-start(bf16[144,1280]{1,0:T(8,128)(2,1)S(1)} %collective-permute-done.25.refs_27_), channel_id=1, source_target_pairs={{0,390},{1,391},{2,384},{3,385},{4,386},{5,387},{6,388},{7,389},{8... | collective-permute-start | bytes 1105928 | tf_op jit(solution)/shard_map/ppermute | solution.py:336
  163.6 4.6 %collective-permute-start.28 = (bf16[144,1280]{1,0:T(8,128)(2,1)}, bf16[144,1280]{1,0:T(8,128)(2,1)}, u32[]{:S(2)}, u32[]{:S(2)}) collective-permute-start(bf16[144,1280]{1,0:T(8,128)(2,1)} %collective-permute-done.24.refs_26_), channel_id=1, source_target_pairs={{0,390},{1,391},{2,384},{3,385},{4,386},{5,387},{6,388},{7,389},{8... | collective-permute-start | bytes 1105928 | tf_op jit(solution)/shard_map/ppermute | solution.py:336
  171.6 4.8 %collective-permute-start.31 = (bf16[144,1280]{1,0:T(8,128)(2,1)}, bf16[144,1280]{1,0:T(8,128)(2,1)}, u32[]{:S(2)}, u32[]{:S(2)}) collective-permute-start(bf16[144,1280]{1,0:T(8,128)(2,1)} %collective-permute-done.29.refs_31_), channel_id=1, source_target_pairs={{0,390},{1,391},{2,384},{3,385},{4,386},{5,387},{6,388},{7,389},{8... | collective-permute-start | bytes 1105928 | tf_op jit(solution)/shard_map/ppermute | solution.py:338
  178.4 7.0 %collective-permute-done.30.refs_32_ = bf16[144,1280]{1,0:T(8,128)(2,1)} collective-permute-done((bf16[144,1280]{1,0:T(8,128)(2,1)}, bf16[144,1280]{1,0:T(8,128)(2,1)}, u32[]{:S(2)}, u32[]{:S(2)}) %collective-permute-start.30) | collective-permute-done | bytes 368672 | tf_op jit(solution)/shard_map/ppermute | solution.py:338
  186.3 14.0 %shard_map.87 = bf16[256,2944]{1,0:T(8,128)(2,1)} custom-call(bf16[256,2944]{1,0:T(8,128)(2,1)} %bitcast.11, bf16[256,2816]{1,0:T(8,128)(2,1)} %bitcast.13, bf16[144,1280]{1,0:T(8,128)(2,1)} %copy-done.4, bf16[144,1280]{1,0:T(8,128)(2,1)} %copy-done.5, bf16[144,1280]{1,0:T(8,128)(2,1)} %copy-done.6, bf16[144,1280]{1,0:T(8,128)(2,1)} %copy-done.8, ...), custom_call_target="tpu_custom_call" | custom-call | tf_op jit(solution)/shard_map/pallas_call | solution.py:212
  200.3 8.5 %all-to-all-start.2 = ((bf16[32,8,2944]{2,1,0:T(8,128)(2,1)}), bf16[32,8,2944]{2,1,0:T(8,128)(2,1)S(1)}, u32[]{:S(2)}, u32[]{:S(2)}) async-start(bf16[32,8,2944]{2,1,0:T(8,128)(2,1)} %bitcast.12), calls=%async_computation.2 | async-start | bytes 3014656 | tf_op jit(solution)/shard_map/all_to_all | solution.py:319
  209.0 21.3 %all-to-all-done.2 = bf16[32,8,2944]{2,1,0:T(8,128)(2,1)S(1)} async-done(((bf16[32,8,2944]{2,1,0:T(8,128)(2,1)}), bf16[32,8,2944]{2,1,0:T(8,128)(2,1)S(1)}, u32[]{:S(2)}, u32[]{:S(2)}) %all-to-all-start.2) | async-done | bytes 1507360 | tf_op jit(solution)/shard_map/all_to_all | solution.py:319
  230.3 2.0 shard_map.88
  (89 shorter events, 33.8 us)
Async XLA Ops:
  1.9 25.5 %collective-permute-start = (bf16[144,1280]{1,0:T(8,128)(2,1)S(1)}, bf16[144,1280]{1,0:T(8,128)(2,1)S(1)}, u32[]{:S(2)}, u32[]{:S(2)}) collective-permute-start(bf16[144,1280]{1,0:T(8,128)(2,1)S(1)} %get-tuple-element.19), channel_id=1, source_target_pairs={{0,260},{1,261},{2,294},{3,295},{4,320},{5,321},{6,354},{7,355},{8... | collective-permute-start | bytes 1105928 | tf_op jit(solution)/shard_map/ppermute | solution.py:329
  17.3 20.6 %collective-permute-start.1 = (bf16[144,1280]{1,0:T(8,128)(2,1)S(1)}, bf16[144,1280]{1,0:T(8,128)(2,1)S(1)}, u32[]{:S(2)}, u32[]{:S(2)}) collective-permute-start(bf16[144,1280]{1,0:T(8,128)(2,1)S(1)} %get-tuple-element.18), channel_id=1, source_target_pairs={{0,260},{1,261},{2,294},{3,295},{4,320},{5,321},{6,354},{7,355},{8... | collective-permute-start | bytes 1105928 | tf_op jit(solution)/shard_map/ppermute | solution.py:329
  27.5 42.8 %collective-permute-start.2 = (bf16[144,1280]{1,0:T(8,128)(2,1)S(1)}, bf16[144,1280]{1,0:T(8,128)(2,1)S(1)}, u32[]{:S(2)}, u32[]{:S(2)}) collective-permute-start(bf16[144,1280]{1,0:T(8,128)(2,1)S(1)} %collective-permute-done.refs_2_), channel_id=1, source_target_pairs={{0,128},{1,129},{2,130},{3,131},{4,132},{5,133},{6,134},{7,135},{8... | collective-permute-start | bytes 1105928 | tf_op jit(solution)/shard_map/ppermute | solution.py:335
  37.9 34.4 %collective-permute-start.5 = (bf16[144,1280]{1,0:T(8,128)(2,1)S(1)}, bf16[144,1280]{1,0:T(8,128)(2,1)S(1)}, u32[]{:S(2)}, u32[]{:S(2)}) collective-permute-start(bf16[144,1280]{1,0:T(8,128)(2,1)S(1)} %collective-permute-done.1.refs_3_), channel_id=1, source_target_pairs={{0,390},{1,391},{2,384},{3,385},{4,386},{5,387},{6,388},{7,389},{8... | collective-permute-start | bytes 1105928 | tf_op jit(solution)/shard_map/ppermute | solution.py:336
  50.8 72.2 %all-to-all-start = ((bf16[32,8,2944]{2,1,0:T(8,128)(2,1)}), bf16[32,8,2944]{2,1,0:T(8,128)(2,1)S(1)}, u32[]{:S(2)}, u32[]{:S(2)}) async-start(bf16[32,8,2944]{2,1,0:T(8,128)(2,1)} %bitcast.14), calls=%async_computation | async-start | bytes 3014656 | tf_op jit(solution)/shard_map/all_to_all | solution.py:319
  70.3 14.4 %collective-permute-start.6 = (bf16[144,1280]{1,0:T(8,128)(2,1)S(1)}, bf16[144,1280]{1,0:T(8,128)(2,1)S(1)}, u32[]{:S(2)}, u32[]{:S(2)}) collective-permute-start(bf16[144,1280]{1,0:T(8,128)(2,1)S(1)} %collective-permute-done.2.refs_4_), channel_id=1, source_target_pairs={{0,128},{1,129},{2,130},{3,131},{4,132},{5,133},{6,134},{7,135},{8... | collective-permute-start | bytes 1105928 | tf_op jit(solution)/shard_map/ppermute | solution.py:335
  72.3 14.4 %collective-permute-start.9 = (bf16[144,1280]{1,0:T(8,128)(2,1)S(1)}, bf16[144,1280]{1,0:T(8,128)(2,1)S(1)}, u32[]{:S(2)}, u32[]{:S(2)}) collective-permute-start(bf16[144,1280]{1,0:T(8,128)(2,1)S(1)} %collective-permute-done.5.refs_7_), channel_id=1, source_target_pairs={{0,390},{1,391},{2,384},{3,385},{4,386},{5,387},{6,388},{7,389},{8... | collective-permute-start | bytes 1105928 | tf_op jit(solution)/shard_map/ppermute | solution.py:336
  76.9 15.8 %collective-permute-start.7 = (bf16[144,1280]{1,0:T(8,128)(2,1)S(1)}, bf16[144,1280]{1,0:T(8,128)(2,1)S(1)}, u32[]{:S(2)}, u32[]{:S(2)}) collective-permute-start(bf16[144,1280]{1,0:T(8,128)(2,1)S(1)} %collective-permute-done.3.refs_5_), channel_id=1, source_target_pairs={{0,128},{1,129},{2,130},{3,131},{4,132},{5,133},{6,134},{7,135},{8... | collective-permute-start | bytes 1105928 | tf_op jit(solution)/shard_map/ppermute | solution.py:335
  78.8 15.7 %collective-permute-start.8 = (bf16[144,1280]{1,0:T(8,128)(2,1)S(1)}, bf16[144,1280]{1,0:T(8,128)(2,1)S(1)}, u32[]{:S(2)}, u32[]{:S(2)}) collective-permute-start(bf16[144,1280]{1,0:T(8,128)(2,1)S(1)} %collective-permute-done.4.refs_6_), channel_id=1, source_target_pairs={{0,390},{1,391},{2,384},{3,385},{4,386},{5,387},{6,388},{7,389},{8... | collective-permute-start | bytes 1105928 | tf_op jit(solution)/shard_map/ppermute | solution.py:336
  84.7 15.8 %collective-permute-start.10 = (bf16[144,1280]{1,0:T(8,128)(2,1)S(1)}, bf16[144,1280]{1,0:T(8,128)(2,1)S(1)}, u32[]{:S(2)}, u32[]{:S(2)}) collective-permute-start(bf16[144,1280]{1,0:T(8,128)(2,1)S(1)} %collective-permute-done.6.refs_8_), channel_id=1, source_target_pairs={{0,128},{1,129},{2,130},{3,131},{4,132},{5,133},{6,134},{7,135},{8... | collective-permute-start | bytes 1105928 | tf_op jit(solution)/shard_map/ppermute | solution.py:335
  86.7 15.8 %collective-permute-start.13 = (bf16[144,1280]{1,0:T(8,128)(2,1)S(1)}, bf16[144,1280]{1,0:T(8,128)(2,1)S(1)}, u32[]{:S(2)}, u32[]{:S(2)}) collective-permute-start(bf16[144,1280]{1,0:T(8,128)(2,1)S(1)} %collective-permute-done.9.refs_11_), channel_id=1, source_target_pairs={{0,390},{1,391},{2,384},{3,385},{4,386},{5,387},{6,388},{7,389},{8... | collective-permute-start | bytes 1105928 | tf_op jit(solution)/shard_map/ppermute | solution.py:336
  92.6 15.9 %collective-permute-start.11 = (bf16[144,1280]{1,0:T(8,128)(2,1)S(1)}, bf16[144,1280]{1,0:T(8,128)(2,1)}, u32[]{:S(2)}, u32[]{:S(2)}) collective-permute-start(bf16[144,1280]{1,0:T(8,128)(2,1)S(1)} %collective-permute-done.7.refs_9_), channel_id=1, source_target_pairs={{0,128},{1,129},{2,130},{3,131},{4,132},{5,133},{6,134},{7,135},{8... | collective-permute-start | bytes 1105928 | tf_op jit(solution)/shard_map/ppermute | solution.py:335
  94.6 15.9 %collective-permute-start.12 = (bf16[144,1280]{1,0:T(8,128)(2,1)S(1)}, bf16[144,1280]{1,0:T(8,128)(2,1)}, u32[]{:S(2)}, u32[]{:S(2)}) collective-permute-start(bf16[144,1280]{1,0:T(8,128)(2,1)S(1)} %collective-permute-done.8.refs_10_), channel_id=1, source_target_pairs={{0,390},{1,391},{2,384},{3,385},{4,386},{5,387},{6,388},{7,389},{8... | collective-permute-start | bytes 1105928 | tf_op jit(solution)/shard_map/ppermute | solution.py:336
  100.5 15.9 %collective-permute-start.14 = (bf16[144,1280]{1,0:T(8,128)(2,1)S(1)}, bf16[144,1280]{1,0:T(8,128)(2,1)}, u32[]{:S(2)}, u32[]{:S(2)}) collective-permute-start(bf16[144,1280]{1,0:T(8,128)(2,1)S(1)} %collective-permute-done.10.refs_12_), channel_id=1, source_target_pairs={{0,128},{1,129},{2,130},{3,131},{4,132},{5,133},{6,134},{7,135},{8... | collective-permute-start | bytes 1105928 | tf_op jit(solution)/shard_map/ppermute | solution.py:335
  102.5 15.9 %collective-permute-start.17 = (bf16[144,1280]{1,0:T(8,128)(2,1)S(1)}, bf16[144,1280]{1,0:T(8,128)(2,1)}, u32[]{:S(2)}, u32[]{:S(2)}) collective-permute-start(bf16[144,1280]{1,0:T(8,128)(2,1)S(1)} %collective-permute-done.13.refs_15_), channel_id=1, source_target_pairs={{0,390},{1,391},{2,384},{3,385},{4,386},{5,387},{6,388},{7,389},{8... | collective-permute-start | bytes 1105928 | tf_op jit(solution)/shard_map/ppermute | solution.py:336
  108.5 24.0 %collective-permute-start.15 = (bf16[144,1280]{1,0:T(8,128)(2,1)}, bf16[144,1280]{1,0:T(8,128)(2,1)}, u32[]{:S(2)}, u32[]{:S(2)}) collective-permute-start(bf16[144,1280]{1,0:T(8,128)(2,1)} %collective-permute-done.11.refs_13_), channel_id=1, source_target_pairs={{0,128},{1,129},{2,130},{3,131},{4,132},{5,133},{6,134},{7,135},{8... | collective-permute-start | bytes 1105928 | tf_op jit(solution)/shard_map/ppermute | solution.py:335
  110.5 24.0 %collective-permute-start.16 = (bf16[144,1280]{1,0:T(8,128)(2,1)}, bf16[144,1280]{1,0:T(8,128)(2,1)}, u32[]{:S(2)}, u32[]{:S(2)}) collective-permute-start(bf16[144,1280]{1,0:T(8,128)(2,1)} %collective-permute-done.12.refs_14_), channel_id=1, source_target_pairs={{0,390},{1,391},{2,384},{3,385},{4,386},{5,387},{6,388},{7,389},{8... | collective-permute-start | bytes 1105928 | tf_op jit(solution)/shard_map/ppermute | solution.py:336
  116.4 22.6 %collective-permute-start.18 = (bf16[144,1280]{1,0:T(8,128)(2,1)}, bf16[144,1280]{1,0:T(8,128)(2,1)}, u32[]{:S(2)}, u32[]{:S(2)}) collective-permute-start(bf16[144,1280]{1,0:T(8,128)(2,1)} %collective-permute-done.14.refs_16_), channel_id=1, source_target_pairs={{0,128},{1,129},{2,130},{3,131},{4,132},{5,133},{6,134},{7,135},{8... | collective-permute-start | bytes 1105928 | tf_op jit(solution)/shard_map/ppermute | solution.py:335
  118.4 22.6 %collective-permute-start.21 = (bf16[144,1280]{1,0:T(8,128)(2,1)}, bf16[144,1280]{1,0:T(8,128)(2,1)}, u32[]{:S(2)}, u32[]{:S(2)}) collective-permute-start(bf16[144,1280]{1,0:T(8,128)(2,1)} %collective-permute-done.17.refs_19_), channel_id=1, source_target_pairs={{0,390},{1,391},{2,384},{3,385},{4,386},{5,387},{6,388},{7,389},{8... | collective-permute-start | bytes 1105928 | tf_op jit(solution)/shard_map/ppermute | solution.py:336
  123.1 53.3 %all-to-all-start.1 = ((bf16[32,8,2816]{2,1,0:T(8,128)(2,1)}), bf16[32,8,2816]{2,1,0:T(8,128)(2,1)S(1)}, u32[]{:S(2)}, u32[]{:S(2)}) async-start(bf16[32,8,2816]{2,1,0:T(8,128)(2,1)} %bitcast.15), calls=%async_computation.1 | async-start | bytes 2883584 | tf_op jit(solution)/shard_map/all_to_all | solution.py:319
  132.5 13.3 %collective-permute-start.19 = (bf16[144,1280]{1,0:T(8,128)(2,1)}, bf16[144,1280]{1,0:T(8,128)(2,1)S(1)}, u32[]{:S(2)}, u32[]{:S(2)}) collective-permute-start(bf16[144,1280]{1,0:T(8,128)(2,1)} %collective-permute-done.15.refs_17_), channel_id=1, source_target_pairs={{0,128},{1,129},{2,130},{3,131},{4,132},{5,133},{6,134},{7,135},{8... | collective-permute-start | bytes 1105928 | tf_op jit(solution)/shard_map/ppermute | solution.py:335
  139.1 14.6 %collective-permute-start.22 = (bf16[144,1280]{1,0:T(8,128)(2,1)}, bf16[144,1280]{1,0:T(8,128)(2,1)S(1)}, u32[]{:S(2)}, u32[]{:S(2)}) collective-permute-start(bf16[144,1280]{1,0:T(8,128)(2,1)} %collective-permute-done.18.refs_20_), channel_id=1, source_target_pairs={{0,128},{1,129},{2,130},{3,131},{4,132},{5,133},{6,134},{7,135},{8... | collective-permute-start | bytes 1105928 | tf_op jit(solution)/shard_map/ppermute | solution.py:335
  141.0 14.6 %collective-permute-start.25 = (bf16[144,1280]{1,0:T(8,128)(2,1)}, bf16[144,1280]{1,0:T(8,128)(2,1)S(1)}, u32[]{:S(2)}, u32[]{:S(2)}) collective-permute-start(bf16[144,1280]{1,0:T(8,128)(2,1)} %collective-permute-done.21.refs_23_), channel_id=1, source_target_pairs={{0,390},{1,391},{2,384},{3,385},{4,386},{5,387},{6,388},{7,389},{8... | collective-permute-start | bytes 1105928 | tf_op jit(solution)/shard_map/ppermute | solution.py:336
  145.8 15.9 %collective-permute-start.23 = (bf16[144,1280]{1,0:T(8,128)(2,1)S(1)}, bf16[144,1280]{1,0:T(8,128)(2,1)}, u32[]{:S(2)}, u32[]{:S(2)}) collective-permute-start(bf16[144,1280]{1,0:T(8,128)(2,1)S(1)} %collective-permute-done.19.refs_21_), channel_id=1, source_target_pairs={{0,128},{1,129},{2,130},{3,131},{4,132},{5,133},{6,134},{7,135},{8... | collective-permute-start | bytes 1105928 | tf_op jit(solution)/shard_map/ppermute | solution.py:335
  147.8 15.9 %collective-permute-start.24 = (bf16[144,1280]{1,0:T(8,128)(2,1)S(1)}, bf16[144,1280]{1,0:T(8,128)(2,1)}, u32[]{:S(2)}, u32[]{:S(2)}) collective-permute-start(bf16[144,1280]{1,0:T(8,128)(2,1)S(1)} %collective-permute-done.20.refs_22_), channel_id=1, source_target_pairs={{0,390},{1,391},{2,384},{3,385},{4,386},{5,387},{6,388},{7,389},{8... | collective-permute-start | bytes 1105928 | tf_op jit(solution)/shard_map/ppermute | solution.py:336
  153.7 15.9 %collective-permute-start.26 = (bf16[144,1280]{1,0:T(8,128)(2,1)S(1)}, bf16[144,1280]{1,0:T(8,128)(2,1)}, u32[]{:S(2)}, u32[]{:S(2)}) collective-permute-start(bf16[144,1280]{1,0:T(8,128)(2,1)S(1)} %collective-permute-done.22.refs_24_), channel_id=1, source_target_pairs={{0,128},{1,129},{2,130},{3,131},{4,132},{5,133},{6,134},{7,135},{8... | collective-permute-start | bytes 1105928 | tf_op jit(solution)/shard_map/ppermute | solution.py:335
  155.7 15.9 %collective-permute-start.29 = (bf16[144,1280]{1,0:T(8,128)(2,1)S(1)}, bf16[144,1280]{1,0:T(8,128)(2,1)}, u32[]{:S(2)}, u32[]{:S(2)}) collective-permute-start(bf16[144,1280]{1,0:T(8,128)(2,1)S(1)} %collective-permute-done.25.refs_27_), channel_id=1, source_target_pairs={{0,390},{1,391},{2,384},{3,385},{4,386},{5,387},{6,388},{7,389},{8... | collective-permute-start | bytes 1105928 | tf_op jit(solution)/shard_map/ppermute | solution.py:336
  161.7 15.8 %collective-permute-start.27 = (bf16[144,1280]{1,0:T(8,128)(2,1)}, bf16[144,1280]{1,0:T(8,128)(2,1)}, u32[]{:S(2)}, u32[]{:S(2)}) collective-permute-start(bf16[144,1280]{1,0:T(8,128)(2,1)} %collective-permute-done.23.refs_25_), channel_id=1, source_target_pairs={{0,128},{1,129},{2,130},{3,131},{4,132},{5,133},{6,134},{7,135},{8... | collective-permute-start | bytes 1105928 | tf_op jit(solution)/shard_map/ppermute | solution.py:335
  163.6 14.7 %collective-permute-start.28 = (bf16[144,1280]{1,0:T(8,128)(2,1)}, bf16[144,1280]{1,0:T(8,128)(2,1)}, u32[]{:S(2)}, u32[]{:S(2)}) collective-permute-start(bf16[144,1280]{1,0:T(8,128)(2,1)} %collective-permute-done.24.refs_26_), channel_id=1, source_target_pairs={{0,390},{1,391},{2,384},{3,385},{4,386},{5,387},{6,388},{7,389},{8... | collective-permute-start | bytes 1105928 | tf_op jit(solution)/shard_map/ppermute | solution.py:336
  169.6 15.8 %collective-permute-start.30 = (bf16[144,1280]{1,0:T(8,128)(2,1)}, bf16[144,1280]{1,0:T(8,128)(2,1)}, u32[]{:S(2)}, u32[]{:S(2)}) collective-permute-start(bf16[144,1280]{1,0:T(8,128)(2,1)} %collective-permute-done.26.refs_28_), channel_id=1, source_target_pairs={{0,128},{1,129},{2,130},{3,131},{4,132},{5,133},{6,134},{7,135},{8... | collective-permute-start | bytes 1105928 | tf_op jit(solution)/shard_map/ppermute | solution.py:338
  171.6 14.7 %collective-permute-start.31 = (bf16[144,1280]{1,0:T(8,128)(2,1)}, bf16[144,1280]{1,0:T(8,128)(2,1)}, u32[]{:S(2)}, u32[]{:S(2)}) collective-permute-start(bf16[144,1280]{1,0:T(8,128)(2,1)} %collective-permute-done.29.refs_31_), channel_id=1, source_target_pairs={{0,390},{1,391},{2,384},{3,385},{4,386},{5,387},{6,388},{7,389},{8... | collective-permute-start | bytes 1105928 | tf_op jit(solution)/shard_map/ppermute | solution.py:338
  200.3 29.9 %all-to-all-start.2 = ((bf16[32,8,2944]{2,1,0:T(8,128)(2,1)}), bf16[32,8,2944]{2,1,0:T(8,128)(2,1)S(1)}, u32[]{:S(2)}, u32[]{:S(2)}) async-start(bf16[32,8,2944]{2,1,0:T(8,128)(2,1)} %bitcast.12), calls=%async_computation.2 | async-start | bytes 3014656 | tf_op jit(solution)/shard_map/all_to_all | solution.py:319
  (25 other events, 751.3 us)
